TPU v7x, 512 devices: a whole 4x4x16 slice. The times are simulated.
512 devices in a mesh: head: 8 (over x, core), ctx: 64 (over z, y).
Axes of the slice: x: 4, y: 4, z: 16, core: 2. Of those that a mesh axis runs over, the one named last changes fastest.
Arguments:
- queries: bfloat16 [32768, 32, 128], P('ctx', 'head'), may hold values from -1.75 to 1.75
- keys: bfloat16 [32768, 32, 128], P('ctx', 'head'), may hold values from -1.75 to 1.75
- values: bfloat16 [32768, 32, 128], P('ctx', 'head'), may hold values from -6 to 6
- out_grad: bfloat16 [32768, 32, 128], P('ctx', 'head'), may hold values from -6 to 6
- gain: float32 [32, 128], P('head'), may hold values from 0.25 to 1.75
- decay_rate: float32 [32], P('head'), may hold values from 1e-05 to 0.03
- doc_lengths: int32 [128], replicated, may hold values from 1 to 4096, 32768 in all
Outputs:
- q_grad: bfloat16 [32768, 32, 128], P('ctx', 'head')
- k_grad: bfloat16 [32768, 32, 128], P('ctx', 'head')
- v_grad: bfloat16 [32768, 32, 128], P('ctx', 'head')
Inputs may be any that keep to these rules, and one draw needn't show every extreme that they name: `doc_lengths`: the lengths sum to 32768 and the longest is exactly 4096.
All inputs are finite; a program needn't handle non-finite values.
Results may differ from a plain program's by a relative error of at most 0.006.
Values sent between devices are 32-bit elements; how exact they have to be, the bound alone decides.
A program may use at most 64 MiB of HBM per device.

v0:
```python
from functools import partial

import jax
import jax.numpy as jnp
from jax import lax
from jax.sharding import PartitionSpec as P

epsilon = 1e-06


def prefix(part, axis, combine, identity, reverse):
    count = lax.axis_size(axis)
    place = lax.axis_index(axis)
    ahead = count - 1 - place if reverse else place
    gathered = jax.tree.map(lambda a: lax.all_gather(a, axis), part)
    state = jax.tree.map(lambda a, e: jnp.zeros_like(a) + jnp.asarray(e, a.dtype), part, identity)

    def one(hop, state):
        source = count - 1 - hop if reverse else hop
        return combine(
            state, jax.tree.map(lambda a: lax.dynamic_index_in_dim(a, source, 0, False), gathered)
        )

    return lax.fori_loop(0, ahead, one, state)


def mix(form, left, right):
    return jnp.einsum(
        form,
        left.astype(jnp.float32),
        right.astype(jnp.float32),
        preferred_element_type=jnp.float32,
    )


def segment_of(starts, positions):
    before = (starts[None, :] <= positions[:, None]).astype(jnp.int32)
    return jnp.sum(before, axis=1) - 1


def decay_mask(segment, decays):
    block_len = segment.shape[0]
    offsets = jnp.arange(block_len, dtype=jnp.int32)
    distance = offsets[:, None] - offsets[None, :]
    allowed = (distance >= 0) & (segment[:, None] == segment[None, :])
    weight = jnp.exp(-decays[:, None, None] * jnp.maximum(distance, 0).astype(jnp.float32)[None])
    return jnp.where(allowed[None], weight, jnp.float32(0.0))


def forward_block(decays, carry, block):
    carried, prev_seg = carry
    queries_blk, key_blk, values_blk, segment = block
    block_len = segment.shape[0]
    offsets = jnp.arange(block_len, dtype=jnp.float32)
    weight = decay_mask(segment, decays)
    scores = mix("thd,shd->hts", queries_blk, key_blk)
    weighted = (scores * weight).astype(jnp.bfloat16)
    output = mix("hts,shd->thd", weighted, values_blk)
    in_factor = jnp.where(
        (segment == prev_seg)[:, None],
        jnp.exp(-decays[None, :] * (offsets[:, None] + 1.0)),
        jnp.float32(0.0),
    )
    output = output + in_factor[:, :, None] * mix(
        "thd,hde->the", queries_blk, carried.astype(jnp.bfloat16)
    )
    last_seg = segment[-1]
    tail = jnp.where(
        (segment == last_seg)[:, None],
        jnp.exp(-decays[None, :] * (block_len - 1.0 - offsets)[:, None]),
        jnp.float32(0.0),
    )
    own_part = mix("shd,she->hde", (key_blk * tail[:, :, None]).astype(jnp.bfloat16), values_blk)
    keep_factor = jnp.where(prev_seg == last_seg, jnp.exp(-decays * block_len), jnp.float32(0.0))
    return (
        (keep_factor[:, None, None] * carried + own_part, last_seg),
        (output, carried, weighted),
    )


def gradient_block(decays, block):
    queries_blk, key_blk, values_blk, grad_blk, segment, carried, prev_seg, weighted = block
    block_len = segment.shape[0]
    offsets = jnp.arange(block_len, dtype=jnp.float32)
    weight = decay_mask(segment, decays)
    grad_scores = mix("thd,shd->hts", grad_blk, values_blk)
    grad_weights = (grad_scores * weight).astype(jnp.bfloat16)
    q_part = mix("hts,shd->thd", grad_weights, key_blk)
    k_part = mix("hts,thd->shd", grad_weights, queries_blk)
    v_part = mix("hts,thd->shd", weighted, grad_blk)
    in_factor = jnp.where(
        (segment == prev_seg)[:, None],
        jnp.exp(-decays[None, :] * (offsets[:, None] + 1.0)),
        jnp.float32(0.0),
    )
    q_part = q_part + in_factor[:, :, None] * mix(
        "the,hde->thd", grad_blk, carried.astype(jnp.bfloat16)
    )
    return (q_part, k_part, v_part)


def reverse_block(decays, carry, block):
    carried, next_seg = carry
    queries_blk, key_blk, values_blk, grad_blk, segment = block
    block_len = segment.shape[0]
    offsets = jnp.arange(block_len, dtype=jnp.float32)
    in_factor = jnp.where(
        (segment == next_seg)[:, None],
        jnp.exp(-decays[None, :] * (block_len - offsets[:, None])),
        jnp.float32(0.0),
    )
    packed = carried.astype(jnp.bfloat16)
    k_extra = in_factor[:, :, None] * mix("she,hde->shd", values_blk, packed)
    v_extra = in_factor[:, :, None] * mix("shd,hde->she", key_blk, packed)
    first_seg = segment[0]
    lead = jnp.where(
        (segment == first_seg)[:, None],
        jnp.exp(-decays[None, :] * offsets[:, None]),
        jnp.float32(0.0),
    )
    own_part = mix("thd,the->hde", (queries_blk * lead[:, :, None]).astype(jnp.bfloat16), grad_blk)
    keep_factor = jnp.where(first_seg == next_seg, jnp.exp(-decays * block_len), jnp.float32(0.0))
    return ((keep_factor[:, None, None] * carried + own_part, first_seg), (k_extra, v_extra))


def in_blocks(array, blocks):
    return array.reshape((blocks, array.shape[0] // blocks) + array.shape[1:])


def chain_combine(earlier, latter):
    return (earlier[0] * latter[0], latter[0][:, None, None] * earlier[1] + latter[1])


def local(queries, keys, values, out_grad, gain, decay_rate, doc_lengths):
    tok_rows, head_count, head_dim = queries.shape
    block_len = min(512, tok_rows)
    blocks = tok_rows // block_len
    norm_width = head_count * head_dim * lax.axis_size("head")
    first_row = lax.axis_index("ctx") * tok_rows
    starts = jnp.cumsum(doc_lengths) - doc_lengths
    positions = first_row + jnp.arange(tok_rows, dtype=jnp.int32)
    segment = segment_of(starts, positions)
    prev_seg = segment_of(starts, jnp.reshape(first_row - 1, (1,)))[0]
    next_seg = segment_of(starts, jnp.reshape(first_row + tok_rows, (1,)))[0]
    offsets = jnp.arange(tok_rows, dtype=jnp.float32)
    query_b = in_blocks(queries, blocks)
    key_b = in_blocks(keys, blocks)
    value_b = in_blocks(values, blocks)
    seg_b = in_blocks(segment, blocks)
    zero_state = jnp.zeros((head_count, head_dim, head_dim), jnp.float32)
    identity = (jnp.ones((head_count,), jnp.float32), zero_state)
    shard_fade = jnp.exp(-decay_rate * tok_rows)
    (own_state, last_seg), (outs_local, entry_states, weighted_b) = lax.scan(
        partial(forward_block, decay_rate), (zero_state, prev_seg), (query_b, key_b, value_b, seg_b)
    )
    forward_summary = (jnp.where(prev_seg == segment[-1], shard_fade, jnp.float32(0.0)), own_state)
    forward_in = prefix(forward_summary, "ctx", chain_combine, identity, False)
    state_in = forward_in[1].astype(jnp.bfloat16)
    in_factor = jnp.where(
        (segment == prev_seg)[:, None],
        jnp.exp(-decay_rate[None, :] * (offsets[:, None] + 1.0)),
        jnp.float32(0.0),
    )
    attn_out = outs_local.reshape(tok_rows, head_count, head_dim)
    attn_out = attn_out + in_factor[:, :, None] * mix("thd,hde->the", queries, state_in)
    gained = gain[None] * out_grad.astype(jnp.float32)
    squares = jnp.sum(attn_out * attn_out, axis=(1, 2))
    cross = jnp.sum(gained * attn_out, axis=(1, 2))
    squares, cross = lax.psum((squares, cross), "head")
    inverse = 1.0 / jnp.sqrt(squares / norm_width + epsilon)
    grad_o = (
        gained * inverse[:, None, None]
        - attn_out * (cross * inverse * inverse * inverse / norm_width)[:, None, None]
    ).astype(jnp.bfloat16)
    grad_b = in_blocks(grad_o, blocks)
    (own_grad, first_seg), (k_extra, v_extra) = lax.scan(
        partial(reverse_block, decay_rate),
        (zero_state, next_seg),
        (query_b, key_b, value_b, grad_b, seg_b),
        reverse=True,
    )
    gradient_summary = (jnp.where(segment[0] == next_seg, shard_fade, jnp.float32(0.0)), own_grad)
    gradient_in = prefix(gradient_summary, "ctx", chain_combine, identity, True)
    prev_blocks = jnp.concatenate([jnp.reshape(prev_seg, (1,)), seg_b[:-1, -1]])
    q_part, k_part, v_part = lax.map(
        partial(gradient_block, decay_rate),
        (query_b, key_b, value_b, grad_b, seg_b, entry_states, prev_blocks, weighted_b),
    )
    shape = (tok_rows, head_count, head_dim)
    q_grad = q_part.reshape(shape) + in_factor[:, :, None] * mix("the,hde->thd", grad_o, state_in)
    back_factor = jnp.where(
        (segment == next_seg)[:, None],
        jnp.exp(-decay_rate[None, :] * (tok_rows - offsets[:, None])),
        jnp.float32(0.0),
    )
    packed = gradient_in[1].astype(jnp.bfloat16)
    k_grad = (k_part + k_extra).reshape(shape) + back_factor[:, :, None] * mix(
        "she,hde->shd", values, packed
    )
    v_grad = (v_part + v_extra).reshape(shape) + back_factor[:, :, None] * mix(
        "shd,hde->she", keys, packed
    )
    return (q_grad.astype(jnp.bfloat16), k_grad.astype(jnp.bfloat16), v_grad.astype(jnp.bfloat16))


def solution(mesh):
    in_specs = (
        P("ctx", "head", None),
        P("ctx", "head", None),
        P("ctx", "head", None),
        P("ctx", "head", None),
        P("head", None),
        P("head"),
        P(),
    )
    out_specs = (P("ctx", "head", None), P("ctx", "head", None), P("ctx", "head", None))
    return jax.shard_map(local, mesh=mesh, in_specs=in_specs, out_specs=out_specs, check_vma=False)
```

profile of v0, /device:TPU:1, one launch (start us, length us, event | category | flops | bytes accessed | tf_op | source)
XLA Modules:
  0.0 572.5 jit_solution(2190166789906831636)
XLA Ops:
  8.4 1.3 fusion.46
  13.2 1.3 broadcast_compare_fusion
  14.5 1.3 dynamic-slice.11
  17.4 1.7 multiply_convert_fusion.3
  19.1 2.1 convolution_add_fusion.1
  22.0 123.6 %all-reduce.2 = (f32[256]{0:T(256)S(1)}, f32[256]{0:T(256)S(1)}) all-reduce(f32[256]{0:T(256)S(1)} %get-tuple-element.288, f32[256]{0:T(256)S(1)} %fusion.52), channel_id=2, replica_groups=mesh['head'=8,'ctx'=64] {'ctx'}, use_global_device_ids=true, to_apply=%add | all-reduce | flops 512 | bytes 4096
  145.9 1.1 copy.121
  147.5 1.4 multiply_convert_fusion.2
  148.9 1.3 multiply_convert_fusion.1
  151.0 1.3 fusion.15
  152.4 68.0 %all-gather.7.cloned.1.call-done = f32[256,128,128]{2,1,0:T(8,128)} async-done(((f32[4,128,128]{2,1,0:T(8,128)}), f32[256,128,128]{2,1,0:T(8,128)}) %all-gather.7.cloned.1.call-update) | async-done | bytes 16777232 | tf_op jit(solution)/shard_map/all_gather | solution.py:15
  220.4 2.7 multiply_reduce_fusion.1
  223.2 12.9 %all-reduce.3 = (f32[512]{0:T(512)S(1)}, f32[512]{0:T(512)S(1)}) all-reduce(f32[512]{0:T(512)S(1)} %get-tuple-element.251, f32[512]{0:T(512)S(1)} %get-tuple-element.250), channel_id=1, replica_groups=mesh['head'=8,'ctx'=64] {'head'}, use_global_device_ids=true, to_apply=%region_8.9 | all-reduce | flops 1024 | bytes 8192 | tf_op jit(solution)/shard_map/psum | solution.py:169
  236.1 1.6 subtract_convert_fusion
  237.7 2.1 convolution_add_fusion
  240.0 2.8 multiply_convert_fusion
  242.8 1.3 copy-done
  245.3 1.1 fusion.16
  246.3 2.1 copy.155
  249.3 2.4 fusion.6
  252.7 238.8 %all-gather.9.cloned.1.call-done = f32[256,128,128]{2,1,0:T(8,128)} async-done(((f32[4,128,128]{2,1,0:T(8,128)}), f32[256,128,128]{2,1,0:T(8,128)}) %all-gather.9.cloned.1.call-update) | async-done | bytes 16777232 | tf_op jit(solution)/shard_map/all_gather | solution.py:15
  491.5 69.4 %while.17 = (s32[]{:T(128)}, f32[4,128,128]{2,1,0:T(8,128)S(1)}, s32[]{:T(128)}, f32[64,4]{1,0:T(8,128)S(1)}, f32[64,4,128,128]{3,2,1,0:T(8,128)}, /*index=5*/s32[]{:T(128)}, s32[]{:T(128)}, s32[]{:T(128)}, s32[]{:T(128)}) while((s32[]{:T(128)}, f32[4,128,128]{2,1,0:T(8,128)S(1)}, s32[]{:T(128)}, f32[64,4]{1,0:T(8,128)S(1)}, ...), condition=%wide.region_11.12_spmd, body=%wide.region_10.11_spmd.sunk | while | flops 131078 | bytes 786635 | solution.py:24
  491.5 1.1 bitcast_add_fusion.5
  492.6 1.1 bitcast_add_fusion.5
  494.8 1.1 bitcast_add_fusion.5
  497.0 1.1 bitcast_add_fusion.5
  498.1 1.1 bitcast_add_fusion.5
  500.3 1.1 bitcast_add_fusion.5
  501.4 1.1 bitcast_add_fusion.5
  503.6 1.1 bitcast_add_fusion.5
  505.8 1.1 bitcast_add_fusion.5
  506.9 1.1 bitcast_add_fusion.5
  509.1 1.1 bitcast_add_fusion.5
  510.2 1.1 bitcast_add_fusion.5
  512.4 1.1 bitcast_add_fusion.5
  513.5 1.1 bitcast_add_fusion.5
  515.7 1.1 bitcast_add_fusion.5
  517.9 1.1 bitcast_add_fusion.5
  519.0 1.1 bitcast_add_fusion.5
  521.2 1.1 bitcast_add_fusion.5
  522.3 1.1 bitcast_add_fusion.5
  524.5 1.1 bitcast_add_fusion.5
  526.7 1.1 bitcast_add_fusion.5
  527.8 1.1 bitcast_add_fusion.5
  530.0 1.1 bitcast_add_fusion.5
  561.2 1.6 fusion.17
  562.8 1.2 copy.157
  564.5 1.2 copy.156
  (163 shorter events, 52.2 us)
Async XLA Ops:
  7.2 141.7 %copy-start.3 = (bf16[512,4,128]{2,1,0:T(4,128)(2,1)S(1)}, bf16[512,4,128]{2,1,0:T(4,128)(2,1)}, u32[]{:S(2)}) copy-start(bf16[512,4,128]{2,1,0:T(4,128)(2,1)} %param.12) | copy-start | bytes 1572868
  7.2 138.8 %copy-start.10 = (bf16[512,4,128]{2,1,0:T(4,128)(2,1)S(1)}, bf16[512,4,128]{2,1,0:T(4,128)(2,1)}, u32[]{:S(2)}) copy-start(bf16[512,4,128]{2,1,0:T(4,128)(2,1)} %param.14) | copy-start | bytes 1572868
  7.2 140.2 %copy-start.2 = (bf16[512,4,128]{2,1,0:T(4,128)(2,1)S(1)}, bf16[512,4,128]{2,1,0:T(4,128)(2,1)}, u32[]{:S(2)}) copy-start(bf16[512,4,128]{2,1,0:T(4,128)(2,1)} %param.11) | copy-start | bytes 1572868
  7.2 213.2 %all-gather.7.cloned.1.call-start = ((), (), s32[]{:S(2)}) async-start(), calls=%async_computation | async-start | bytes 17039360 | tf_op jit(solution)/shard_map/all_gather | solution.py:15
  21.2 470.2 %all-gather.9.cloned.1.call-start = ((), (), s32[]{:S(2)}) async-start(), calls=%async_computation.1 | async-start | bytes 17039360 | tf_op jit(solution)/shard_map/all_gather | solution.py:15
  147.2 3.0 copy-start.9
  147.4 2.7 copy-start.11
  147.4 2.7 copy-start.6
  151.0 69.4 %copy-start.8 = (bf16[512,4,128]{0,2,1:T(8,128)(2,1)S(1)}, bf16[512,4,128]{0,2,1:T(8,128)(2,1)}, u32[]{:S(2)}) copy-start(bf16[512,4,128]{0,2,1:T(8,128)(2,1)} %copy.121) | copy-start | bytes 1572868
  151.0 69.4 %copy-start.12 = (f32[4,128]{1,0:T(4,128)S(1)}, f32[4,128]{1,0:T(4,128)}, u32[]{:S(2)}) copy-start(f32[4,128]{1,0:T(4,128)} %param.15) | copy-start | bytes 6148
  239.9 4.2 copy-start.4
  242.8 1.3 copy-start
  248.4 3.3 copy-start.1
  251.8 309.1 %copy-start.7 = (bf16[512,4,128]{2,1,0:T(4,128)(2,1)S(1)}, bf16[512,4,128]{2,1,0:T(4,128)(2,1)}, u32[]{:S(2)}) copy-start(bf16[512,4,128]{2,1,0:T(4,128)(2,1)} %param.13) | copy-start | bytes 1572868
  251.8 309.5 %copy-start.5 = (bf16[512,4,128]{2,1,0:T(4,128)(2,1)S(1)}, bf16[512,4,128]{2,1,0:T(4,128)(2,1)}, u32[]{:S(2)}) copy-start(bf16[512,4,128]{2,1,0:T(4,128)(2,1)} %param.12) | copy-start | bytes 1572868
Sparse Core Ops, SparseCore 0:
  21.3 199.0 all-gather.6
  240.0 251.4 all-gather.8
where the time goes:
time: 575 us; the launch traced here: 572 us
  waiting for transfers between devices  307 us (53%)
  blocking collectives  137 us (24%)
  other arithmetic  76.6 us (13%)
  matrix products  22 us (4%)
  between operations  17.7 us (3%)
  local copies, waits for them, and re-layouts  10.8 us (2%)
    all_gather x2, waiting for transfers between devices, prefix(): gathered = jax.tree.map(lambda a: lax.all_gather(a, axis), part)  307 us
    unnamed x1, blocking collectives  124 us
    add x63, other arithmetic, chain_combine(): latter[0][:, None, None] * earlier[1] + latter[1]  66.8 us
    dot_general x16, matrix products, mix(): jnp.einsum(form, left.astype(jnp.float32), right.astype(jnp.float32), pre...  22 us
    psum x1, blocking collectives, local(): squares, cross = lax.psum((squares, cross), 'head')  12.9 us
  transfers between devices with their start and end apart: 2, of which 2 were waited for; matrix products, arithmetic and copies ran while one was open for 3% of the time, Pallas kernels for 0%

commit v1 on v0

--- a/solution.py
+++ b/solution.py
@@ -137,7 +137,8 @@
     blocks = tok_rows // block_len
     norm_width = head_count * head_dim * lax.axis_size("head")
     first_row = lax.axis_index("ctx") * tok_rows
-    starts = jnp.cumsum(doc_lengths) - doc_lengths
+    order = jnp.arange(doc_lengths.shape[0], dtype=jnp.int32)
+    starts = jnp.sum(jnp.where(order[None, :] < order[:, None], doc_lengths[None, :], 0), axis=1)
     positions = first_row + jnp.arange(tok_rows, dtype=jnp.int32)
     segment = segment_of(starts, positions)
     prev_seg = segment_of(starts, jnp.reshape(first_row - 1, (1,)))[0]

time: 575 us -> 574 us (level)
  no operation moved by 1% of the time
where the time goes in v1:
time: 574 us; the launch traced here: 572 us
  waiting for transfers between devices  306 us (53%)
  blocking collectives  137 us (24%)
  other arithmetic  76.5 us (13%)
  matrix products  22.1 us (4%)
  between operations  17.7 us (3%)
  local copies, waits for them, and re-layouts  11.2 us (2%)
    all_gather x2, waiting for transfers between devices, prefix(): gathered = jax.tree.map(lambda a: lax.all_gather(a, axis), part)  306 us
    unnamed x1, blocking collectives  124 us
    add x63, other arithmetic, chain_combine(): latter[0][:, None, None] * earlier[1] + latter[1]  66.8 us
    dot_general x16, matrix products, mix(): jnp.einsum(form, left.astype(jnp.float32), right.astype(jnp.float32), pre...  22.1 us
    psum x1, blocking collectives, local(): squares, cross = lax.psum((squares, cross), 'head')  12.9 us
  transfers between devices with their start and end apart: 2, of which 2 were waited for; matrix products, arithmetic and copies ran while one was open for 3% of the time, Pallas kernels for 0%

profile of v1, /device:TPU:1, one launch (start us, length us, event | category | flops | bytes accessed | tf_op | source)
XLA Modules:
  0.0 571.7 jit_solution(16359751838763262843)
XLA Ops:
  12.2 1.3 broadcast_compare_fusion
  13.5 1.3 dynamic-slice.11
  16.5 1.7 multiply_convert_fusion.3
  18.1 2.1 convolution_add_fusion.1
  21.1 123.6 %all-reduce.2 = (f32[256]{0:T(256)S(1)}, f32[256]{0:T(256)S(1)}) all-reduce(f32[256]{0:T(256)S(1)} %get-tuple-element.287, f32[256]{0:T(256)S(1)} %fusion.52), channel_id=2, replica_groups=mesh['head'=8,'ctx'=64] {'ctx'}, use_global_device_ids=true, to_apply=%add | all-reduce | flops 512 | bytes 4096
  145.0 2.1 copy.118
  147.5 1.4 multiply_convert_fusion.2
  148.9 1.3 multiply_convert_fusion.1
  151.1 1.3 fusion.15
  152.4 67.0 %all-gather.7.cloned.1.call-done = f32[256,128,128]{2,1,0:T(8,128)} async-done(((f32[4,128,128]{2,1,0:T(8,128)}), f32[256,128,128]{2,1,0:T(8,128)}) %all-gather.7.cloned.1.call-update) | async-done | bytes 16777232 | tf_op jit(solution)/shard_map/all_gather | solution.py:15
  219.5 2.8 multiply_reduce_fusion.1
  222.3 12.9 %all-reduce.3 = (f32[512]{0:T(512)S(1)}, f32[512]{0:T(512)S(1)}) all-reduce(f32[512]{0:T(512)S(1)} %get-tuple-element.251, f32[512]{0:T(512)S(1)} %get-tuple-element.250), channel_id=1, replica_groups=mesh['head'=8,'ctx'=64] {'head'}, use_global_device_ids=true, to_apply=%region_8.9 | all-reduce | flops 1024 | bytes 8192 | tf_op jit(solution)/shard_map/psum | solution.py:170
  235.2 1.6 subtract_convert_fusion
  236.8 2.1 convolution_add_fusion
  239.0 2.9 multiply_convert_fusion
  241.9 1.3 copy-done
  244.4 1.1 fusion.16
  245.4 2.1 copy.151
  248.4 2.4 fusion.6
  251.8 238.7 %all-gather.9.cloned.1.call-done = f32[256,128,128]{2,1,0:T(8,128)} async-done(((f32[4,128,128]{2,1,0:T(8,128)}), f32[256,128,128]{2,1,0:T(8,128)}) %all-gather.9.cloned.1.call-update) | async-done | bytes 16777232 | tf_op jit(solution)/shard_map/all_gather | solution.py:15
  490.5 69.5 %while.17 = (s32[]{:T(128)}, f32[4,128,128]{2,1,0:T(8,128)S(1)}, s32[]{:T(128)}, f32[64,4]{1,0:T(8,128)S(1)}, f32[64,4,128,128]{3,2,1,0:T(8,128)}, /*index=5*/s32[]{:T(128)}, s32[]{:T(128)}, s32[]{:T(128)}, s32[]{:T(128)}) while((s32[]{:T(128)}, f32[4,128,128]{2,1,0:T(8,128)S(1)}, s32[]{:T(128)}, f32[64,4]{1,0:T(8,128)S(1)}, ...), condition=%wide.region_11.12_spmd, body=%wide.region_10.11_spmd.sunk | while | flops 131078 | bytes 786635 | solution.py:24
  490.5 1.1 bitcast_add_fusion.5
  491.7 1.1 bitcast_add_fusion.5
  492.8 1.1 bitcast_add_fusion.5
  495.0 1.1 bitcast_add_fusion.5
  496.1 1.1 bitcast_add_fusion.5
  497.2 1.1 bitcast_add_fusion.5
  500.5 1.1 bitcast_add_fusion.5
  501.6 1.1 bitcast_add_fusion.5
  502.7 1.1 bitcast_add_fusion.5
  506.0 1.1 bitcast_add_fusion.5
  507.1 1.1 bitcast_add_fusion.5
  508.2 1.1 bitcast_add_fusion.5
  511.5 1.1 bitcast_add_fusion.5
  512.6 1.1 bitcast_add_fusion.5
  513.7 1.1 bitcast_add_fusion.5
  515.9 1.1 bitcast_add_fusion.5
  517.0 1.1 bitcast_add_fusion.5
  518.1 1.1 bitcast_add_fusion.5
  521.5 1.1 bitcast_add_fusion.5
  522.6 1.1 bitcast_add_fusion.5
  523.7 1.1 bitcast_add_fusion.5
  527.0 1.1 bitcast_add_fusion.5
  528.1 1.1 bitcast_add_fusion.5
  529.2 1.1 bitcast_add_fusion.5
  560.4 1.6 fusion.17
  562.0 1.2 copy.153
  563.7 1.2 copy.152
  (159 shorter events, 51.6 us)
Async XLA Ops:
  7.2 141.7 %copy-start.3 = (bf16[512,4,128]{2,1,0:T(4,128)(2,1)S(1)}, bf16[512,4,128]{2,1,0:T(4,128)(2,1)}, u32[]{:S(2)}) copy-start(bf16[512,4,128]{2,1,0:T(4,128)(2,1)} %param.12) | copy-start | bytes 1572868
  7.2 140.3 %copy-start.2 = (bf16[512,4,128]{2,1,0:T(4,128)(2,1)S(1)}, bf16[512,4,128]{2,1,0:T(4,128)(2,1)}, u32[]{:S(2)}) copy-start(bf16[512,4,128]{2,1,0:T(4,128)(2,1)} %param.11) | copy-start | bytes 1572868
  7.2 212.3 %all-gather.7.cloned.1.call-start = ((), (), s32[]{:S(2)}) async-start(), calls=%async_computation | async-start | bytes 17039360 | tf_op jit(solution)/shard_map/all_gather | solution.py:15
  20.3 470.2 %all-gather.9.cloned.1.call-start = ((), (), s32[]{:S(2)}) async-start(), calls=%async_computation.1 | async-start | bytes 17039360 | tf_op jit(solution)/shard_map/all_gather | solution.py:15
  147.2 3.0 copy-start.9
  147.5 2.7 copy-start.10
  147.5 2.7 copy-start.6
  151.1 68.4 %copy-start.8 = (bf16[512,4,128]{0,2,1:T(8,128)(2,1)S(1)}, bf16[512,4,128]{0,2,1:T(8,128)(2,1)}, u32[]{:S(2)}) copy-start(bf16[512,4,128]{0,2,1:T(8,128)(2,1)} %copy.118) | copy-start | bytes 1572868
  151.1 68.4 %copy-start.11 = (f32[4,128]{1,0:T(4,128)S(1)}, f32[4,128]{1,0:T(4,128)}, u32[]{:S(2)}) copy-start(f32[4,128]{1,0:T(4,128)} %param.15) | copy-start | bytes 6148
  239.0 4.2 copy-start.4
  241.9 1.4 copy-start
  247.6 3.3 copy-start.1
  250.9 309.2 %copy-start.7 = (bf16[512,4,128]{2,1,0:T(4,128)(2,1)S(1)}, bf16[512,4,128]{2,1,0:T(4,128)(2,1)}, u32[]{:S(2)}) copy-start(bf16[512,4,128]{2,1,0:T(4,128)(2,1)} %param.13) | copy-start | bytes 1572868
  250.9 309.6 %copy-start.5 = (bf16[512,4,128]{2,1,0:T(4,128)(2,1)S(1)}, bf16[512,4,128]{2,1,0:T(4,128)(2,1)}, u32[]{:S(2)}) copy-start(bf16[512,4,128]{2,1,0:T(4,128)(2,1)} %param.12) | copy-start | bytes 1572868
Sparse Core Ops, SparseCore 0:
  20.4 199.0 all-gather.6
  239.0 251.4 all-gather.8

commit v2 on v0

v2 whole, which is shorter than its diff:
```python
import functools

import jax
import jax.numpy as jnp
from jax import lax
from jax.experimental import pallas as pl
from jax.experimental.pallas import tpu as pltpu
from jax.sharding import PartitionSpec as P

epsilon = 1e-06
BLK = 512
GROUP = 4
FEAT = 128
HPD = 4
FAR = 1e37
f32 = jnp.float32
bf16 = jnp.bfloat16
PARTS = ((0, 256, 0), (256, 512, 256))


def nn(a, b):
    return lax.dot_general(a, b, (((1,), (0,)), ((), ())), preferred_element_type=f32)


def nt(a, b):
    return lax.dot_general(a, b, (((1,), (1,)), ((), ())), preferred_element_type=f32)


def kernel(
    zs, hs, total, width,
    q_hbm, k_hbm, v_hbm, g_hbm, gain_ref, rate_ref, lens_ref,
    qo_hbm, ko_hbm, vo_hbm,
    qin, kin, vin, gin, st_q, st_k, st_v, st_g,
    qh, kh, vh, qT, kT, vT, gT, dist, decay, probsT, oT, goT,
    fown, frec, fsum, fin, fout, fent,
    bown, brec, bsum, bin_, bout, bent,
    stat, stats, kacc, vacc, backc, so_q, so_k, so_v, oq, ok, ov,
    in_sem, out_sem, a_s, a_r, t_s, t_r, e_s, e_r, n_s, n_r, c_s, c_r, u_s, u_r, w_s, w_r,
):
    head = lax.axis_index("head")
    ctx = lax.axis_index("ctx")
    z = ctx // GROUP
    y = ctx % GROUP

    def row_dev(d):
        return {"ctx": z * GROUP + (y + d) % GROUP}

    def col_dev(d):
        return {"ctx": ((z + d + zs) % zs) * GROUP + y}

    def head_dev(m):
        return {"head": (head + m) % hs}

    loads = [
        pltpu.make_async_copy(s, t, in_sem.at[i])
        for i, (s, t) in enumerate(((k_hbm, kin), (v_hbm, vin), (q_hbm, qin), (g_hbm, gin)))
    ]
    for c in loads:
        c.start()
    barrier = pltpu.get_barrier_semaphore()
    peers = [row_dev(d) for d in range(1, GROUP)]
    peers += [col_dev(d) for d in (-2, -1, 1, 2)]
    peers += [head_dev(m) for m in range(1, hs)]
    for p in peers:
        pl.semaphore_signal(barrier, inc=1, device_id=p, device_id_type=pl.DeviceIdType.MESH)

    b0 = (ctx * BLK).astype(f32)
    g0 = (z * (BLK * GROUP)).astype(f32)
    lens = jnp.broadcast_to(lens_ref[...].astype(f32), (128, 128))
    low = lax.broadcasted_iota(jnp.int32, (128, 128), 0) < lax.broadcasted_iota(jnp.int32, (128, 128), 1)
    starts = jnp.sum(jnp.where(low, lens.T, 0.0), axis=0, keepdims=True)
    starts_c = jnp.broadcast_to(starts, (128, 128)).T
    t_row = lax.broadcasted_iota(jnp.int32, (1, BLK), 1).astype(f32)
    own_start = jnp.concatenate(
        [
            jnp.max(
                jnp.where(starts_c - b0 <= t_row[:, i : i + 128], starts_c - b0, -2.0 * total),
                axis=0, keepdims=True,
            )
            for i in range(0, BLK, 128)
        ],
        axis=1,
    )

    def start_of(position):
        found = jnp.max(jnp.where(starts <= position, starts, -1.0), axis=1, keepdims=True)
        found = jnp.broadcast_to(found, (8, 128))
        return jnp.where(position >= total, f32(total), found)

    idx = lax.broadcasted_iota(jnp.int32, (8, 128), 0)
    idxf = idx.astype(f32)
    ends = start_of(jnp.where(idx == 5, b0 + (BLK - 1.0), g0 + idxf * BLK - 1.0))
    firsts = start_of(jnp.where(idx == 5, b0 + BLK, jnp.where(idx == 6, g0 + 2.0 * BLK * GROUP, g0 + idxf * BLK)))
    end_g = ends - g0
    first_g = firsts - g0
    last_start = ends[5:6, 0:1] - b0
    next_start = firsts[5:6, :] - b0

    rate_y = rate_ref[0, y]
    in_mask = own_start < 0.0
    tail_mask = t_row >= last_start
    lead_mask = own_start <= 0.0

    def in_row(h):
        return jnp.where(in_mask, jnp.exp(-rate_ref[0, h] * (t_row + 1.0)), 0.0)

    def split_heads(source, stage):
        stage[...] = source[...].astype(f32)

    def of_head(stage, h):
        return stage[pl.ds(h, BLK, stride=HPD), :]

    loads[0].wait()
    split_heads(kin, st_k)
    loads[1].wait()
    split_heads(vin, st_v)
    a_copies = []
    for d in (1, 2, 3, 0):
        h = (y + d) % GROUP
        k_f = of_head(st_k, h)
        k_t = k_f.T
        kh[h] = k_f.astype(bf16)
        kT[h] = k_t.astype(bf16)
        v_f = of_head(st_v, h)
        vh[h] = v_f.astype(bf16)
        tail = jnp.where(tail_mask, jnp.exp(-rate_ref[0, h] * (BLK - 1.0 - t_row)), 0.0)
        fown[h] = nn((k_t * tail).astype(bf16), v_f.astype(bf16))
        if d == 1:
            pl.semaphore_wait(barrier, len(peers))
        if d:
            c = pltpu.make_async_remote_copy(
                src_ref=fown.at[h], dst_ref=frec.at[d], send_sem=a_s.at[d], recv_sem=a_r.at[d],
                device_id=row_dev(d), device_id_type=pl.DeviceIdType.MESH,
            )
            c.start()
            a_copies.append(c)

    loads[2].wait()
    split_heads(qin, st_q)
    loads[3].wait()
    split_heads(gin, st_g)
    gain_c = jnp.concatenate([gain_ref[...], jnp.zeros((FEAT - HPD, FEAT), f32)], axis=0).T

    s_col = lax.broadcasted_iota(jnp.int32, (BLK, BLK), 0).astype(f32)
    t_col = lax.broadcasted_iota(jnp.int32, (BLK, BLK), 1).astype(f32)
    dist[...] = jnp.where((s_col <= t_col) & (s_col >= own_start), t_col - s_col, FAR)

    def prepare(h):
        q_f = of_head(st_q, h)
        qh[h] = q_f.astype(bf16)
        qT[h] = q_f.T.astype(bf16)
        gT[h] = of_head(st_g, h).T * gain_c[:, h : h + 1]
        vT[h] = vh[h].astype(f32).T.astype(bf16)
        s_i = lax.broadcasted_iota(jnp.int32, (BLK, FEAT), 0).astype(f32)
        backc[h] = jnp.where(s_i >= next_start, jnp.exp(-rate_ref[0, h] * (BLK - s_i)), 0.0)

    def forward(h):
        prepare(h)
        for s0, s1, t0 in PARTS:
            w = jnp.exp(-rate_ref[0, h] * dist[s0:s1, t0:])
            decay[h, s0:s1, t0:] = w
            probsT[h, s0:s1, t0:] = (nn(kh[h, s0:s1, :], qT[h, :, t0:]) * w).astype(bf16)
        oT[h, :, 0:256] = nn(vT[h, :, 0:256], probsT[h, 0:256, 0:256])
        oT[h, :, 256:512] = nn(vT[h], probsT[h, :, 256:512])

    def fade(mask, count):
        return jnp.where(mask, jnp.exp(-rate_y * (BLK * jnp.maximum(count, 0.0))), 0.0)

    forward(0)
    for c in a_copies:
        c.wait()
    inner = [None] * (GROUP + 1)
    for d in range(GROUP):
        j = (y + GROUP - d) % GROUP
        jf = j.astype(f32)
        coef = fade((idx > j) & (end_g <= BLK * (jf + 1.0) - 1.0), idxf - 1.0 - jf)
        part = fown[y] if d == 0 else frec[d]
        for i in range(1, GROUP + 1):
            term = coef[i : i + 1, :] * part
            inner[i] = term if inner[i] is None else inner[i] + term
    fsum[...] = inner[GROUP]
    t_copies = []
    for n in (1, 0):
        c = pltpu.make_async_remote_copy(
            src_ref=fsum, dst_ref=fin.at[n], send_sem=t_s.at[n], recv_sem=t_r.at[n],
            device_id=col_dev(n + 1), device_id_type=pl.DeviceIdType.MESH,
        )
        c.start()
        t_copies.append(c)
    for i in range(1, GROUP):
        fout[i] = inner[i]

    forward(1)
    forward(2)
    for c in t_copies:
        c.wait()
    far = fade(end_g <= -BLK * GROUP - 1.0, jnp.full((8, 128), GROUP, f32))[0:1, :]
    enter = fin[0] + far * fin[1]
    carry = fade(end_g <= -1.0, idxf)
    fout[0] = enter
    for i in range(1, GROUP):
        fout[i] = fout[i] + carry[i : i + 1, :] * enter
    e_copies = []
    for d in (1, 2, 3):
        c = pltpu.make_async_remote_copy(
            src_ref=fout.at[(y + d) % GROUP], dst_ref=fent.at[y], send_sem=e_s.at[d], recv_sem=e_r.at[d],
            device_id=row_dev(d), device_id_type=pl.DeviceIdType.MESH,
        )
        c.start()
        e_copies.append(c)
    fent[y] = fout[y]
    forward(3)
    for c in e_copies:
        c.wait()

    squares = jnp.zeros((8, BLK), f32)
    cross = jnp.zeros((8, BLK), f32)
    for h in range(HPD):
        state = fent[h].T.astype(bf16)
        o = oT[h] + in_row(h) * nn(state, qT[h])
        oT[h] = o
        squares = squares + jnp.sum((o * o).reshape(FEAT // 8, 8, BLK), axis=0)
        cross = cross + jnp.sum((o * gT[h]).reshape(FEAT // 8, 8, BLK), axis=0)
    squares = jnp.sum(squares, axis=0, keepdims=True)
    cross = jnp.sum(cross, axis=0, keepdims=True)
    for i in range(4):
        stat[i : i + 1, :] = squares[:, i * 128 : (i + 1) * 128]
        stat[i + 4 : i + 5, :] = cross[:, i * 128 : (i + 1) * 128]
    n_copies = []
    for m in range(1, hs):
        c = pltpu.make_async_remote_copy(
            src_ref=stat, dst_ref=stats.at[m], send_sem=n_s.at[m], recv_sem=n_r.at[m],
            device_id=head_dev(m), device_id_type=pl.DeviceIdType.MESH,
        )
        c.start()
        n_copies.append(c)
    for c in n_copies:
        c.wait()
    both = stat[...]
    for m in range(1, hs):
        both = both + stats[m]
    inverse = 1.0 / jnp.sqrt(both[0:4, :] / width + epsilon)
    factor = both[4:8, :] * inverse * inverse * inverse / width
    inv_row = jnp.concatenate([inverse[i : i + 1, :] for i in range(4)], axis=1)
    fac_row = jnp.concatenate([factor[i : i + 1, :] for i in range(4)], axis=1)

    c_copies = []
    for d in (1, 2, 3, 0):
        h = (y + d) % GROUP
        go = (gT[h] * inv_row - oT[h] * fac_row).astype(bf16)
        goT[h] = go
        lead = jnp.where(lead_mask, jnp.exp(-rate_ref[0, h] * t_row), 0.0)
        bown[h] = nt((qT[h].astype(f32) * lead).astype(bf16), go)
        if d:
            c = pltpu.make_async_remote_copy(
                src_ref=bown.at[h], dst_ref=brec.at[d], send_sem=c_s.at[d], recv_sem=c_r.at[d],
                device_id=row_dev(d), device_id_type=pl.DeviceIdType.MESH,
            )
            c.start()
            c_copies.append(c)

    def backward(h):
        go = goT[h]
        q_t = in_row(h) * nn(fent[h].astype(bf16), go)
        w0 = (nn(vh[h, 0:256, :], go) * decay[h, 0:256, :]).astype(bf16)
        w1 = (nn(vh[h, 256:512, :], go[:, 256:]) * decay[h, 256:512, 256:]).astype(bf16)
        q0 = q_t[:, 0:256] + nn(kT[h, :, 0:256], w0[:, 0:256])
        q1 = q_t[:, 256:] + nn(kT[h, :, 0:256], w0[:, 256:]) + nn(kT[h, :, 256:], w1)
        so_q[pl.ds(h, BLK, stride=HPD), :] = jnp.concatenate([q0.T, q1.T], axis=0)
        kacc[h, 0:256, :] = nn(w0, qh[h])
        kacc[h, 256:512, :] = nn(w1, qh[h, 256:512, :])
        vacc[h, 0:256, :] = nt(probsT[h, 0:256, :], go)
        vacc[h, 256:512, :] = nt(probsT[h, 256:512, 256:], go[:, 256:])

    backward(0)
    for c in c_copies:
        c.wait()
    outer = [None] * GROUP
    group_sum = None
    for d in range(GROUP):
        j = (y + GROUP - d) % GROUP
        jf = j.astype(f32)
        first_j = jnp.sum(jnp.where(idx == j, first_g, 0.0), axis=0, keepdims=True)
        at = jnp.where(idx == 7, 0.0, idxf + 1.0)
        coef = fade((jf >= at) & (first_j <= BLK * at), jf - at)
        part = bown[y] if d == 0 else brec[d]
        for i in range(GROUP - 1):
            term = coef[i : i + 1, :] * part
            outer[i] = term if outer[i] is None else outer[i] + term
        term = coef[7:8, :] * part
        group_sum = term if group_sum is None else group_sum + term
    bsum[...] = group_sum
    u_copies = []
    for n in (1, 0):
        c = pltpu.make_async_remote_copy(
            src_ref=bsum, dst_ref=bin_.at[n], send_sem=u_s.at[n], recv_sem=u_r.at[n],
            device_id=col_dev(-(n + 1)), device_id_type=pl.DeviceIdType.MESH,
        )
        c.start()
        u_copies.append(c)
    for i in range(GROUP - 1):
        bout[i] = outer[i]
    backward(1)
    backward(2)
    for c in u_copies:
        c.wait()
    far = fade(first_g <= BLK * GROUP, jnp.full((8, 128), GROUP, f32))[6:7, :]
    enter = bin_[0] + far * bin_[1]
    carry = fade(first_g[4:5, :] <= BLK * (idxf + 1.0), GROUP - 1.0 - idxf)
    bout[GROUP - 1] = enter
    for i in range(GROUP - 1):
        bout[i] = bout[i] + carry[i : i + 1, :] * enter
    w_copies = []
    for d in (1, 2, 3):
        c = pltpu.make_async_remote_copy(
            src_ref=bout.at[(y + d) % GROUP], dst_ref=bent.at[y], send_sem=w_s.at[d], recv_sem=w_r.at[d],
            device_id=row_dev(d), device_id_type=pl.DeviceIdType.MESH,
        )
        c.start()
        w_copies.append(c)
    bent[y] = bout[y]
    backward(3)
    oq[...] = so_q[...].astype(bf16)
    q_out = pltpu.make_async_copy(oq, qo_hbm, out_sem.at[0])
    q_out.start()
    for c in w_copies:
        c.wait()
    for h in range(HPD):
        state = bent[h].astype(bf16)
        so_k[pl.ds(h, BLK, stride=HPD), :] = kacc[h] + backc[h] * nt(vh[h], state)
        so_v[pl.ds(h, BLK, stride=HPD), :] = vacc[h] + backc[h] * nn(kh[h], state)
    ok[...] = so_k[...].astype(bf16)
    k_out = pltpu.make_async_copy(ok, ko_hbm, out_sem.at[1])
    k_out.start()
    ov[...] = so_v[...].astype(bf16)
    v_out = pltpu.make_async_copy(ov, vo_hbm, out_sem.at[2])
    v_out.start()
    q_out.wait()
    k_out.wait()
    v_out.wait()


def local(zs, hs, queries, keys, values, out_grad, gain, decay_rate, doc_lengths):
    rows = BLK * HPD
    flat = [a.reshape(rows, FEAT) for a in (queries, keys, values, out_grad)]
    hbm = pl.BlockSpec(memory_space=pl.ANY)
    vmem = pl.BlockSpec(memory_space=pltpu.VMEM)
    smem = pl.BlockSpec(memory_space=pltpu.SMEM)
    V = pltpu.VMEM
    mat = (FEAT, FEAT)
    chain = [
        V((HPD,) + mat, f32), V((GROUP,) + mat, f32), V(mat, f32),
        V((2,) + mat, f32), V((GROUP,) + mat, f32), V((HPD,) + mat, f32),
    ]
    scratch = (
        [V((rows, FEAT), bf16)] * 4
        + [V((rows, FEAT), f32)] * 4
        + [V((HPD, BLK, FEAT), bf16)] * 3
        + [V((HPD, FEAT, BLK), bf16)] * 3
        + [V((HPD, FEAT, BLK), f32), V((BLK, BLK), f32), V((HPD, BLK, BLK), f32), V((HPD, BLK, BLK), bf16)]
        + [V((HPD, FEAT, BLK), f32), V((HPD, FEAT, BLK), bf16)]
        + chain + chain
        + [V((8, 128), f32), V((hs, 8, 128), f32)]
        + [V((HPD, BLK, FEAT), f32)] * 3
        + [V((rows, FEAT), f32)] * 3
        + [V((rows, FEAT), bf16)] * 3
    )
    dma = pltpu.SemaphoreType.DMA
    sems = [dma((4,)), dma((3,))]
    sems += [dma((GROUP,)), dma((GROUP,)), dma((2,)), dma((2,)), dma((GROUP,)), dma((GROUP,))]
    sems += [dma((hs,)), dma((hs,))]
    sems += [dma((GROUP,)), dma((GROUP,)), dma((2,)), dma((2,)), dma((GROUP,)), dma((GROUP,))]
    outs = pl.pallas_call(
        functools.partial(kernel, zs, hs, zs * GROUP * BLK, hs * HPD * FEAT),
        out_shape=[jax.ShapeDtypeStruct((rows, FEAT), bf16)] * 3,
        in_specs=[hbm] * 4 + [vmem, smem, vmem],
        out_specs=[hbm] * 3,
        scratch_shapes=scratch + sems,
        compiler_params=pltpu.CompilerParams(
            collective_id=0, has_side_effects=True, vmem_limit_bytes=48 * 2**20
        ),
        cost_estimate=pl.CostEstimate(flops=2 * 10**9, bytes_accessed=4 * 10**6, transcendentals=10**6),
    )(*flat, gain, decay_rate.reshape(1, HPD), doc_lengths.reshape(1, doc_lengths.shape[0]))
    return tuple(o.reshape(BLK, HPD, FEAT) for o in outs)


def solution(mesh):
    spec = P("ctx", "head", None)
    zs, hs = mesh.shape["ctx"] // GROUP, mesh.shape["head"]
    return jax.shard_map(
        functools.partial(local, zs, hs), mesh=mesh,
        in_specs=(spec,) * 4 + (P("head", None), P("head"), P()),
        out_specs=(spec,) * 3, check_vma=False,
    )
```

time: 575 us -> 59 us (0.10)
  waiting for transfers between devices: 307 us -> 0 us
  blocking collectives: 137 us -> 0 us
  other arithmetic: 76.6 us -> 0 us
  Pallas kernels: 0 us -> 50.8 us
  matrix products: 22 us -> 0 us
  between operations: 17.7 us -> 0.67 us
    all_gather x2 -> x0, waiting for transfers between devices: 307 us -> none  [prefix(): gathered = jax.tree.map(lambda a: lax.all_gather(a, axis), part)]
    unnamed x1 -> x0, blocking collectives: 124 us -> none
    add x65 -> x0, other arithmetic: 66.9 us -> none  [the longest x63 66.8 us: chain_combine(): latter[0][:, None, None] * earlier[1] + latter[1]]
    pallas_call x0 -> x1, Pallas kernels: none -> 50.8 us  [local(): pl.pallas_call(functools.partial(kernel, zs, hs, zs * GROUP * BLK, hs * H...]
    dot_general x16 -> x0, matrix products: 22 us -> none  [mix(): jnp.einsum(form, left.astype(jnp.float32), right.astype(jnp.float32), pre...]
    psum x1 -> x0, blocking collectives: 12.9 us -> none  [local(): squares, cross = lax.psum((squares, cross), 'head')]
  transfers between devices with their start and end apart: 2 -> 0, of which waited for: 2 -> 0; matrix products, arithmetic and copies ran while one was open for 3% -> 0% of each run, Pallas kernels for 0% -> 0%
where the time goes in v2:
time: 59 us; the launch traced here: 58.7 us
  Pallas kernels  50.8 us (86%)
  local copies, waits for them, and re-layouts  7.21 us (12%)
  between operations  0.67 us (1%)
    pallas_call x1, Pallas kernels, local(): pl.pallas_call(functools.partial(kernel, zs, hs, zs * GROUP * BLK, hs * H...  50.8 us
    unnamed x17, local copies, waits for them, and re-layouts  7.21 us

profile of v2, /device:TPU:1, one launch (start us, length us, event | category | flops | bytes accessed | tf_op | source)
XLA Modules:
  0.0 58.7 jit_solution(14022414882140318858)
XLA Ops:
  0.6 0.0 copy-start.4
  0.6 0.0 copy-start.5
  0.7 0.0 copy-start.6
  0.7 0.7 %copy-done.4 = f32[4,128]{1,0:T(4,128)S(1)} copy-done((f32[4,128]{1,0:T(4,128)S(1)}, f32[4,128]{1,0:T(4,128)}, u32[]{:S(2)}) %copy-start.4) | copy-done | bytes 2072
  1.3 0.0 copy-done.5
  1.3 0.0 copy-done.6
  1.3 0.0 copy-start
  1.3 1.0 %copy-done = bf16[512,4,128]{2,1,0:T(4,128)(2,1)S(1)} copy-done((bf16[512,4,128]{2,1,0:T(4,128)(2,1)S(1)}, bf16[512,4,128]{2,1,0:T(4,128)(2,1)}, u32[]{:S(2)}) %copy-start) | copy-done | bytes 524312
  2.4 0.0 copy-start.1
  2.4 1.0 %copy-done.1 = bf16[512,4,128]{2,1,0:T(4,128)(2,1)S(1)} copy-done((bf16[512,4,128]{2,1,0:T(4,128)(2,1)S(1)}, bf16[512,4,128]{2,1,0:T(4,128)(2,1)}, u32[]{:S(2)}) %copy-start.1) | copy-done | bytes 524312
  3.4 0.0 copy-start.2
  3.4 1.0 %copy-done.2 = bf16[512,4,128]{2,1,0:T(4,128)(2,1)S(1)} copy-done((bf16[512,4,128]{2,1,0:T(4,128)(2,1)S(1)}, bf16[512,4,128]{2,1,0:T(4,128)(2,1)}, u32[]{:S(2)}) %copy-start.2) | copy-done | bytes 524312
  4.4 0.0 copy-start.3
  4.5 1.0 %copy-done.3 = bf16[512,4,128]{2,1,0:T(4,128)(2,1)S(1)} copy-done((bf16[512,4,128]{2,1,0:T(4,128)(2,1)S(1)}, bf16[512,4,128]{2,1,0:T(4,128)(2,1)}, u32[]{:S(2)}) %copy-start.3) | copy-done | bytes 524312
  5.5 50.8 %shard_map.94 = (bf16[2048,128]{1,0:T(8,128)(2,1)S(1)}, bf16[2048,128]{1,0:T(8,128)(2,1)S(1)}, bf16[2048,128]{1,0:T(8,128)(2,1)S(1)}) custom-call(bf16[2048,128]{1,0:T(8,128)(2,1)S(1)} %bitcast.12, bf16[2048,128]{1,0:T(8,128)(2,1)S(1)} %bitcast.13, bf16[2048,128]{1,0:T(8,128)(2,1)S(1)} %bitcast.14, bf16[2048,128]{1,0:T(8,128)(2,1)S(1)} %bitcast.15, ...), custom_call_target="tpu_custom_call" | custom-call | flops 2000000000 | bytes 4000000 | tf_op jit(solution)/shard_map/pallas_call | solution.py:373
  56.3 0.8 %copy.13 = bf16[512,4,128]{2,1,0:T(4,128)(2,1)} copy(bf16[512,4,128]{2,1,0:T(4,128)(2,1)S(1)} %bitcast.11) | data formatting | bytes 1048576
  57.1 0.8 %copy.14 = bf16[512,4,128]{2,1,0:T(4,128)(2,1)} copy(bf16[512,4,128]{2,1,0:T(4,128)(2,1)S(1)} %bitcast.10) | data formatting | bytes 1048576
  57.9 0.8 %copy.15 = bf16[512,4,128]{2,1,0:T(4,128)(2,1)} copy(bf16[512,4,128]{2,1,0:T(4,128)(2,1)S(1)} %bitcast.9) | data formatting | bytes 1048576
Async XLA Ops:
  0.6 0.7 %copy-start.4 = (f32[4,128]{1,0:T(4,128)S(1)}, f32[4,128]{1,0:T(4,128)}, u32[]{:S(2)}) copy-start(f32[4,128]{1,0:T(4,128)} %gain_ref.1) | copy-start | bytes 6148
  0.6 0.7 %copy-start.5 = (f32[4]{0:T(128)S(1)}, f32[4]{0:T(128)}, u32[]{:S(2)}) copy-start(f32[4]{0:T(128)} %param.12) | copy-start | bytes 52
  0.7 0.7 %copy-start.6 = (s32[128]{0:T(128)S(1)}, s32[128]{0:T(128)}, u32[]{:S(2)}) copy-start(s32[128]{0:T(128)} %param.13) | copy-start | bytes 1540
  1.3 1.0 %copy-start = (bf16[512,4,128]{2,1,0:T(4,128)(2,1)S(1)}, bf16[512,4,128]{2,1,0:T(4,128)(2,1)}, u32[]{:S(2)}) copy-start(bf16[512,4,128]{2,1,0:T(4,128)(2,1)} %param.7) | copy-start | bytes 1572868
  2.4 1.0 %copy-start.1 = (bf16[512,4,128]{2,1,0:T(4,128)(2,1)S(1)}, bf16[512,4,128]{2,1,0:T(4,128)(2,1)}, u32[]{:S(2)}) copy-start(bf16[512,4,128]{2,1,0:T(4,128)(2,1)} %param.8) | copy-start | bytes 1572868
  3.4 1.0 %copy-start.2 = (bf16[512,4,128]{2,1,0:T(4,128)(2,1)S(1)}, bf16[512,4,128]{2,1,0:T(4,128)(2,1)}, u32[]{:S(2)}) copy-start(bf16[512,4,128]{2,1,0:T(4,128)(2,1)} %param.9) | copy-start | bytes 1572868
  4.4 1.0 %copy-start.3 = (bf16[512,4,128]{2,1,0:T(4,128)(2,1)S(1)}, bf16[512,4,128]{2,1,0:T(4,128)(2,1)}, u32[]{:S(2)}) copy-start(bf16[512,4,128]{2,1,0:T(4,128)(2,1)} %param.10) | copy-start | bytes 1572868

commit v3 on v2

v3 whole, which is shorter than its diff:
```python
import functools

import jax
import jax.numpy as jnp
from jax import lax
from jax.experimental import pallas as pl
from jax.experimental.pallas import tpu as pltpu
from jax.sharding import PartitionSpec as P

epsilon = 1e-06
BLK = 512
GROUP = 4
FEAT = 128
HPD = 4
FAR = 1e37
f32 = jnp.float32
bf16 = jnp.bfloat16
PARTS = ((0, 256, 0), (256, 512, 256))
CHUNKS = 4
ROWS = FEAT // CHUNKS


def nn(a, b):
    return lax.dot_general(a, b, (((1,), (0,)), ((), ())), preferred_element_type=f32)


def nt(a, b):
    return lax.dot_general(a, b, (((1,), (1,)), ((), ())), preferred_element_type=f32)


def kernel(
    zs, hs, total, width,
    q_hbm, k_hbm, v_hbm, g_hbm, gain_hbm, rate_hbm, lens_hbm,
    oq, ok, ov,
    qin, kin, vin, gin, st_q, st_k, st_v, st_g,
    qh, kh, vh, qT, kT, vT, gT, dist, decay, probsT, oT, goT,
    fown, frec, fsum, fin, fout, fent,
    bown, brec, bsum, bin_, bout, bent,
    stat, stats, kacc, vacc, backc, so_q, so_k, so_v, gain_ref, rate_ref, lens_ref,
    in_sem, a_s, a_r, t_s, t_r, e_s, e_r, n_s, n_r, c_s, c_r, u_s, u_r, w_s, w_r,
):
    head = lax.axis_index("head")
    ctx = lax.axis_index("ctx")
    z = ctx // GROUP
    y = ctx % GROUP

    def row_dev(d):
        return {"ctx": z * GROUP + (y + d) % GROUP}

    def col_dev(d):
        return {"ctx": ((z + d + zs) % zs) * GROUP + y}

    def head_dev(m):
        return {"head": (head + m) % hs}

    loads = [
        pltpu.make_async_copy(s, t, in_sem.at[i])
        for i, (s, t) in enumerate(
            (
                (k_hbm, kin), (v_hbm, vin), (q_hbm, qin), (g_hbm, gin),
                (lens_hbm, lens_ref), (rate_hbm, rate_ref), (gain_hbm, gain_ref),
            )
        )
    ]
    for c in loads:
        c.start()
    barrier = pltpu.get_barrier_semaphore()
    peers = [row_dev(d) for d in range(1, GROUP)]
    peers += [col_dev(d) for d in (-2, -1, 1, 2)]
    peers += [head_dev(m) for m in range(1, hs)]
    for p in peers:
        pl.semaphore_signal(barrier, inc=1, device_id=p, device_id_type=pl.DeviceIdType.MESH)

    def remote(source, target, sends, receives, device):
        copy = pltpu.make_async_remote_copy(
            src_ref=source, dst_ref=target, send_sem=sends, recv_sem=receives,
            device_id=device, device_id_type=pl.DeviceIdType.MESH,
        )
        copy.start()
        return copy

    def chunk(c):
        return pl.ds(c * ROWS, ROWS)

    def fade(rate, mask, count):
        return jnp.where(mask, jnp.exp(-rate * (BLK * jnp.maximum(count, 0.0))), 0.0)

    for c in loads[4:]:
        c.wait()
    b0 = (ctx * BLK).astype(f32)
    g0 = (z * (BLK * GROUP)).astype(f32)
    lens = jnp.broadcast_to(lens_ref[...].astype(f32), (128, 128))
    low = lax.broadcasted_iota(jnp.int32, (128, 128), 0) < lax.broadcasted_iota(jnp.int32, (128, 128), 1)
    starts = jnp.sum(jnp.where(low, lens.T, 0.0), axis=0, keepdims=True)
    starts_c = jnp.broadcast_to(starts, (128, 128)).T
    t_row = lax.broadcasted_iota(jnp.int32, (1, BLK), 1).astype(f32)
    own_start = jnp.concatenate(
        [
            jnp.max(
                jnp.where(starts_c - b0 <= t_row[:, i : i + 128], starts_c - b0, -2.0 * total),
                axis=0, keepdims=True,
            )
            for i in range(0, BLK, 128)
        ],
        axis=1,
    )

    def start_of(position):
        found = jnp.max(jnp.where(starts <= position, starts, -1.0), axis=1, keepdims=True)
        found = jnp.broadcast_to(found, (8, 128))
        return jnp.where(position >= total, f32(total), found)

    idx = lax.broadcasted_iota(jnp.int32, (8, 128), 0)
    idxf = idx.astype(f32)
    ends = start_of(jnp.where(idx == 5, b0 + (BLK - 1.0), g0 + idxf * BLK - 1.0))
    firsts = start_of(jnp.where(idx == 5, b0 + BLK, jnp.where(idx == 6, g0 + 2.0 * BLK * GROUP, g0 + idxf * BLK)))
    end_g = ends - g0
    first_g = firsts - g0
    last_start = ends[5:6, 0:1] - b0
    next_start = firsts[5:6, :] - b0

    rate_y = rate_ref[0, y]
    in_mask = own_start < 0.0
    tail_mask = t_row >= last_start
    lead_mask = own_start <= 0.0

    def in_row(h):
        return jnp.where(in_mask, jnp.exp(-rate_ref[0, h] * (t_row + 1.0)), 0.0)

    def split_heads(source, stage):
        stage[...] = source[...].astype(f32)

    def of_head(stage, h):
        return stage[pl.ds(h, BLK, stride=HPD), :]

    loads[0].wait()
    split_heads(kin, st_k)
    loads[1].wait()
    split_heads(vin, st_v)
    a_copies = {}
    for d in (2, 1, 3, 0):
        h = (y + d) % GROUP
        k_f = of_head(st_k, h)
        k_t = k_f.T
        kh[h] = k_f.astype(bf16)
        kT[h] = k_t.astype(bf16)
        v_f = of_head(st_v, h)
        vh[h] = v_f.astype(bf16)
        tail = jnp.where(tail_mask, jnp.exp(-rate_ref[0, h] * (BLK - 1.0 - t_row)), 0.0)
        fown[h] = nn((k_t * tail).astype(bf16), v_f.astype(bf16))
        if not a_copies:
            pl.semaphore_wait(barrier, len(peers))
        if d:
            for c in range(CHUNKS):
                a_copies[d, c] = remote(
                    fown.at[h, chunk(c)], frec.at[d, chunk(c)], a_s.at[d, c], a_r.at[d, c], row_dev(d)
                )

    loads[2].wait()
    split_heads(qin, st_q)
    loads[3].wait()
    split_heads(gin, st_g)
    gain_c = jnp.concatenate([gain_ref[...], jnp.zeros((FEAT - HPD, FEAT), f32)], axis=0).T

    s_col = lax.broadcasted_iota(jnp.int32, (BLK, BLK), 0).astype(f32)
    t_col = lax.broadcasted_iota(jnp.int32, (BLK, BLK), 1).astype(f32)
    dist[...] = jnp.where((s_col <= t_col) & (s_col >= own_start), t_col - s_col, FAR)

    def prepare(h):
        q_f = of_head(st_q, h)
        qh[h] = q_f.astype(bf16)
        qT[h] = q_f.T.astype(bf16)
        gT[h] = of_head(st_g, h).T * gain_c[:, h : h + 1]
        vT[h] = vh[h].astype(f32).T.astype(bf16)
        s_i = lax.broadcasted_iota(jnp.int32, (BLK, FEAT), 0).astype(f32)
        backc[h] = jnp.where(s_i >= next_start, jnp.exp(-rate_ref[0, h] * (BLK - s_i)), 0.0)

    def forward(h):
        prepare(h)
        for s0, s1, t0 in PARTS:
            w = jnp.exp(-rate_ref[0, h] * dist[s0:s1, t0:])
            decay[h, s0:s1, t0:] = w
            probsT[h, s0:s1, t0:] = (nn(kh[h, s0:s1, :], qT[h, :, t0:]) * w).astype(bf16)
        oT[h, :, 0:256] = nn(vT[h, :, 0:256], probsT[h, 0:256, 0:256])
        oT[h, :, 256:512] = nn(vT[h], probsT[h, :, 256:512])

    forward(0)
    forward(1)
    source = [(y + GROUP - d) % GROUP for d in range(GROUP)]
    coefs = [
        fade(
            rate_y, (idx > j) & (end_g <= BLK * (j.astype(f32) + 1.0) - 1.0), idxf - 1.0 - j.astype(f32)
        )
        for j in source
    ]
    t_copies = {}
    for c in range(CHUNKS):
        for d in (1, 3, 2):
            a_copies[d, c].wait()
        total_c = coefs[0][GROUP : GROUP + 1, :] * fown[y, chunk(c), :]
        for d in range(1, GROUP):
            total_c = total_c + coefs[d][GROUP : GROUP + 1, :] * frec[d, chunk(c), :]
        fsum[chunk(c), :] = total_c
        for n in (1, 0):
            t_copies[n, c] = remote(
                fsum.at[chunk(c)], fin.at[n, chunk(c)], t_s.at[n, c], t_r.at[n, c], col_dev(n + 1)
            )
    for i in range(1, GROUP):
        inner = coefs[0][i : i + 1, :] * fown[y]
        for d in range(1, GROUP):
            inner = inner + coefs[d][i : i + 1, :] * frec[d]
        fout[i] = inner
    forward(2)
    forward(3)
    far = fade(rate_y, end_g <= -BLK * GROUP - 1.0, jnp.full((8, 128), GROUP, f32))[0:1, :]
    carry = fade(rate_y, end_g <= -1.0, idxf)
    e_copies = {}
    for c in range(CHUNKS):
        for n in (0, 1):
            t_copies[n, c].wait()
        enter = fin[0, chunk(c), :] + far * fin[1, chunk(c), :]
        fout[0, chunk(c), :] = enter
        for i in range(1, GROUP):
            fout[i, chunk(c), :] = fout[i, chunk(c), :] + carry[i : i + 1, :] * enter
        for d in (2, 1, 3):
            e_copies[d, c] = remote(
                fout.at[(y + d) % GROUP, chunk(c)], fent.at[y, chunk(c)], e_s.at[d, c], e_r.at[d, c], row_dev(d)
            )
    fent[y] = fout[y]

    squares = jnp.zeros((8, BLK), f32)
    cross = jnp.zeros((8, BLK), f32)
    for d in (0, 1, 3, 2):
        h = source[d]
        if d:
            for c in range(CHUNKS):
                e_copies[d, c].wait()
        state = fent[h].T.astype(bf16)
        o = oT[h] + in_row(h) * nn(state, qT[h])
        oT[h] = o
        squares = squares + jnp.sum((o * o).reshape(FEAT // 8, 8, BLK), axis=0)
        cross = cross + jnp.sum((o * gT[h]).reshape(FEAT // 8, 8, BLK), axis=0)
    squares = jnp.sum(squares, axis=0, keepdims=True)
    cross = jnp.sum(cross, axis=0, keepdims=True)
    for i in range(4):
        stat[i : i + 1, :] = squares[:, i * 128 : (i + 1) * 128]
        stat[i + 4 : i + 5, :] = cross[:, i * 128 : (i + 1) * 128]
    n_copies = [
        remote(stat, stats.at[m], n_s.at[m], n_r.at[m], head_dev(m))
        for m in sorted(range(1, hs), key=lambda m: abs(m - hs // 2))
    ]
    for c in n_copies:
        c.wait()
    both = stat[...]
    for m in range(1, hs):
        both = both + stats[m]
    inverse = 1.0 / jnp.sqrt(both[0:4, :] / width + epsilon)
    factor = both[4:8, :] * inverse * inverse * inverse / width
    inv_row = jnp.concatenate([inverse[i : i + 1, :] for i in range(4)], axis=1)
    fac_row = jnp.concatenate([factor[i : i + 1, :] for i in range(4)], axis=1)

    c_copies = {}
    for d in (2, 1, 3, 0):
        h = (y + d) % GROUP
        go = (gT[h] * inv_row - oT[h] * fac_row).astype(bf16)
        goT[h] = go
        lead = jnp.where(lead_mask, jnp.exp(-rate_ref[0, h] * t_row), 0.0)
        bown[h] = nt((qT[h].astype(f32) * lead).astype(bf16), go)
        if d:
            for c in range(CHUNKS):
                c_copies[d, c] = remote(
                    bown.at[h, chunk(c)], brec.at[d, chunk(c)], c_s.at[d, c], c_r.at[d, c], row_dev(d)
                )

    def backward(h):
        go = goT[h]
        q_t = in_row(h) * nn(fent[h].astype(bf16), go)
        w0 = (nn(vh[h, 0:256, :], go) * decay[h, 0:256, :]).astype(bf16)
        w1 = (nn(vh[h, 256:512, :], go[:, 256:]) * decay[h, 256:512, 256:]).astype(bf16)
        q0 = q_t[:, 0:256] + nn(kT[h, :, 0:256], w0[:, 0:256])
        q1 = q_t[:, 256:] + nn(kT[h, :, 0:256], w0[:, 256:]) + nn(kT[h, :, 256:], w1)
        so_q[pl.ds(h, BLK, stride=HPD), :] = jnp.concatenate([q0.T, q1.T], axis=0)
        kacc[h, 0:256, :] = nn(w0, qh[h])
        kacc[h, 256:512, :] = nn(w1, qh[h, 256:512, :])
        vacc[h, 0:256, :] = nt(probsT[h, 0:256, :], go)
        vacc[h, 256:512, :] = nt(probsT[h, 256:512, 256:], go[:, 256:])

    backward(0)
    backward(1)
    at = jnp.where(idx == 7, 0.0, idxf + 1.0)
    coefs = []
    for j in source:
        first_j = jnp.sum(jnp.where(idx == j, first_g, 0.0), axis=0, keepdims=True)
        jf = j.astype(f32)
        coefs.append(fade(rate_y, (jf >= at) & (first_j <= BLK * at), jf - at))
    u_copies = {}
    for c in range(CHUNKS):
        for d in (1, 3, 2):
            c_copies[d, c].wait()
        total_c = coefs[0][7:8, :] * bown[y, chunk(c), :]
        for d in range(1, GROUP):
            total_c = total_c + coefs[d][7:8, :] * brec[d, chunk(c), :]
        bsum[chunk(c), :] = total_c
        for n in (1, 0):
            u_copies[n, c] = remote(
                bsum.at[chunk(c)], bin_.at[n, chunk(c)], u_s.at[n, c], u_r.at[n, c], col_dev(-(n + 1))
            )
    for i in range(GROUP - 1):
        outer = coefs[0][i : i + 1, :] * bown[y]
        for d in range(1, GROUP):
            outer = outer + coefs[d][i : i + 1, :] * brec[d]
        bout[i] = outer
    backward(2)
    backward(3)
    oq[...] = so_q[...].astype(bf16)
    far = fade(rate_y, first_g <= BLK * GROUP, jnp.full((8, 128), GROUP, f32))[6:7, :]
    carry = fade(rate_y, first_g[4:5, :] <= BLK * (idxf + 1.0), GROUP - 1.0 - idxf)
    w_copies = {}
    for c in range(CHUNKS):
        for n in (0, 1):
            u_copies[n, c].wait()
        enter = bin_[0, chunk(c), :] + far * bin_[1, chunk(c), :]
        bout[GROUP - 1, chunk(c), :] = enter
        for i in range(GROUP - 1):
            bout[i, chunk(c), :] = bout[i, chunk(c), :] + carry[i : i + 1, :] * enter
        for d in (2, 1, 3):
            w_copies[d, c] = remote(
                bout.at[(y + d) % GROUP, chunk(c)], bent.at[y, chunk(c)], w_s.at[d, c], w_r.at[d, c], row_dev(d)
            )
    bent[y] = bout[y]

    for d in (0, 1, 3, 2):
        h = source[d]
        if d:
            for c in range(CHUNKS):
                w_copies[d, c].wait()
        state = bent[h].astype(bf16)
        so_k[pl.ds(h, BLK, stride=HPD), :] = kacc[h] + backc[h] * nt(vh[h], state)
        so_v[pl.ds(h, BLK, stride=HPD), :] = vacc[h] + backc[h] * nn(kh[h], state)
    ok[...] = so_k[...].astype(bf16)
    ov[...] = so_v[...].astype(bf16)


def copy_out(a, b, c, a_hbm, b_hbm, c_hbm, sems):
    copies = [
        pltpu.make_async_copy(s, t, sems.at[i])
        for i, (s, t) in enumerate(((a, a_hbm), (b, b_hbm), (c, c_hbm)))
    ]
    for x in copies:
        x.start()
    for x in copies:
        x.wait()


def local(zs, hs, queries, keys, values, out_grad, gain, decay_rate, doc_lengths):
    rows = BLK * HPD
    flat = [a.reshape(rows, FEAT) for a in (queries, keys, values, out_grad)]
    hbm = pl.BlockSpec(memory_space=pltpu.HBM)
    vmem = pl.BlockSpec(memory_space=pltpu.VMEM)
    V = pltpu.VMEM
    mat = (FEAT, FEAT)
    chain = [
        V((HPD,) + mat, f32), V((GROUP,) + mat, f32), V(mat, f32),
        V((2,) + mat, f32), V((GROUP,) + mat, f32), V((HPD,) + mat, f32),
    ]
    scratch = (
        [V((rows, FEAT), bf16)] * 4
        + [V((rows, FEAT), f32)] * 4
        + [V((HPD, BLK, FEAT), bf16)] * 3
        + [V((HPD, FEAT, BLK), bf16)] * 3
        + [V((HPD, FEAT, BLK), f32), V((BLK, BLK), f32), V((HPD, BLK, BLK), f32), V((HPD, BLK, BLK), bf16)]
        + [V((HPD, FEAT, BLK), f32), V((HPD, FEAT, BLK), bf16)]
        + chain + chain
        + [V((8, 128), f32), V((hs, 8, 128), f32)]
        + [V((HPD, BLK, FEAT), f32)] * 3
        + [V((rows, FEAT), f32)] * 3
        + [V((HPD, FEAT), f32), pltpu.SMEM((1, HPD), f32), V((1, doc_lengths.shape[0]), jnp.int32)]
    )
    dma = pltpu.SemaphoreType.DMA
    moves = [dma((GROUP, CHUNKS))] * 2 + [dma((2, CHUNKS))] * 2 + [dma((GROUP, CHUNKS))] * 2
    sems = [dma((7,))] + moves + [dma((hs,))] * 2 + moves
    operands = (*flat, gain, decay_rate.reshape(1, HPD), doc_lengths.reshape(1, doc_lengths.shape[0]))
    result = [jax.ShapeDtypeStruct((rows, FEAT), bf16)] * 3
    outs = pl.pallas_call(
        functools.partial(kernel, zs, hs, zs * GROUP * BLK, hs * HPD * FEAT),
        out_shape=[V((rows, FEAT), bf16)] * 3,
        in_specs=[hbm] * 7,
        out_specs=[vmem] * 3,
        scratch_shapes=scratch + sems,
        compiler_params=pltpu.CompilerParams(
            collective_id=0, has_side_effects=True, vmem_limit_bytes=40 * 2**20
        ),
        cost_estimate=pl.CostEstimate(flops=2 * 10**9, bytes_accessed=4 * 10**6, transcendentals=10**6),
    )(*(pltpu.with_memory_space_constraint(a, pltpu.HBM) for a in operands))
    outs = pl.pallas_call(
        copy_out, out_shape=result, in_specs=[vmem] * 3, out_specs=[hbm] * 3, scratch_shapes=[dma((3,))],
        compiler_params=pltpu.CompilerParams(vmem_limit_bytes=2**20),
    )(*outs)
    return tuple(o.reshape(BLK, HPD, FEAT) for o in outs)


def solution(mesh):
    spec = P("ctx", "head", None)
    zs, hs = mesh.shape["ctx"] // GROUP, mesh.shape["head"]
    return jax.shard_map(
        functools.partial(local, zs, hs), mesh=mesh,
        in_specs=(spec,) * 4 + (P("head", None), P("head"), P()),
        out_specs=(spec,) * 3, check_vma=False,
    )
```

time: 59 us -> 48.1 us (0.82); the launches traced: 58.7 us -> 47.2 us
  local copies, waits for them, and re-layouts: 7.21 us -> 0 us
  Pallas kernels: 50.8 us -> 46.5 us
    unnamed x17 -> x0, local copies, waits for them, and re-layouts: 7.21 us -> none
    pallas_call x1, Pallas kernels: 50.8 us -> 45.4 us  [local(): pl.pallas_call(functools.partial(kernel, zs, hs, zs * GROUP * BLK, hs * H...]
    pallas_call x0 -> x1, Pallas kernels: none -> 1.17 us  [local(): pl.pallas_call(copy_out, out_shape=result, in_specs=[vmem] * 3, out_specs...]
where the time goes in v3:
time: 48.1 us; the launch traced here: 47.2 us
  Pallas kernels  46.5 us (97%)
  between operations  0.64 us (1%)
    pallas_call x1, Pallas kernels, local(): pl.pallas_call(functools.partial(kernel, zs, hs, zs * GROUP * BLK, hs * H...  45.4 us
    pallas_call x1, Pallas kernels, local(): pl.pallas_call(copy_out, out_shape=result, in_specs=[vmem] * 3, out_specs...  1.17 us

profile of v3, /device:TPU:1, one launch (start us, length us, event | category | flops | bytes accessed | tf_op | source)
XLA Modules:
  0.0 47.2 jit_solution(16855279370770754969)
XLA Ops:
  0.6 45.4 %shard_map.94 = (bf16[2048,128]{1,0:T(8,128)(2,1)S(1)}, bf16[2048,128]{1,0:T(8,128)(2,1)S(1)}, bf16[2048,128]{1,0:T(8,128)(2,1)S(1)}) custom-call(bf16[2048,128]{1,0:T(8,128)(2,1)} %bitcast.9, bf16[2048,128]{1,0:T(8,128)(2,1)} %bitcast.10, bf16[2048,128]{1,0:T(8,128)(2,1)} %bitcast.11, bf16[2048,128]{1,0:T(8,128)(2,1)} %bitcast.12, f32[4,128]{1,0:T(4,128)} %gain_hbm.1, ...), custom_call_target="tpu_custom_call" | custom-call | flops 2000000000 | bytes 4000000 | tf_op jit(solution)/shard_map/pallas_call | solution.py:384
  46.0 1.2 %shard_map.95 = (bf16[2048,128]{1,0:T(8,128)(2,1)}, bf16[2048,128]{1,0:T(8,128)(2,1)}, bf16[2048,128]{1,0:T(8,128)(2,1)}) custom-call(bf16[2048,128]{1,0:T(8,128)(2,1)S(1)} %get-tuple-element.9.a, bf16[2048,128]{1,0:T(8,128)(2,1)S(1)} %get-tuple-element.10.b, bf16[2048,128]{1,0:T(8,128)(2,1)S(1)} %get-tuple-element.11.c), custom_call_target="tpu_custom_call" | custom-call | tf_op jit(solution)/shard_map/pallas_call | solution.py:395

commit v4 on v3

--- a/solution.py
+++ b/solution.py
@@ -37,7 +37,7 @@
     fown, frec, fsum, fin, fout, fent,
     bown, brec, bsum, bin_, bout, bent,
     stat, stats, kacc, vacc, backc, so_q, so_k, so_v, gain_ref, rate_ref, lens_ref,
-    in_sem, a_s, a_r, t_s, t_r, e_s, e_r, n_s, n_r, c_s, c_r, u_s, u_r, w_s, w_r,
+    in_sem, above, a_s, a_r, t_s, t_r, e_s, e_r, n_s, n_r, c_s, c_r, u_s, u_r, w_s, w_r,
 ):
     head = lax.axis_index("head")
     ctx = lax.axis_index("ctx")
@@ -53,31 +53,65 @@
     def head_dev(m):
         return {"head": (head + m) % hs}
 
+    def signal(semaphore, device):
+        pl.semaphore_signal(semaphore, inc=1, device_id=device, device_id_type=pl.DeviceIdType.MESH)
+
     loads = [
         pltpu.make_async_copy(s, t, in_sem.at[i])
         for i, (s, t) in enumerate(
             (
-                (k_hbm, kin), (v_hbm, vin), (q_hbm, qin), (g_hbm, gin),
-                (lens_hbm, lens_ref), (rate_hbm, rate_ref), (gain_hbm, gain_ref),
+                (k_hbm, kin), (v_hbm, vin), (lens_hbm, lens_ref), (rate_hbm, rate_ref),
+                (q_hbm, qin), (g_hbm, gin), (gain_hbm, gain_ref),
             )
         )
     ]
-    for c in loads:
+    barrier = pltpu.get_barrier_semaphore()
+    for d in (2, 1, 3):
+        signal(barrier, row_dev(d))
+    for c in loads[:4]:
         c.start()
-    barrier = pltpu.get_barrier_semaphore()
-    peers = [row_dev(d) for d in range(1, GROUP)]
-    peers += [col_dev(d) for d in (-2, -1, 1, 2)]
-    peers += [head_dev(m) for m in range(1, hs)]
-    for p in peers:
-        pl.semaphore_signal(barrier, inc=1, device_id=p, device_id_type=pl.DeviceIdType.MESH)
-
-    def remote(source, target, sends, receives, device):
+    for n in (2, 1):
+        @pl.when(z < zs - n)
+        def _(n=n):
+            signal(barrier, col_dev(n))
+    for m in range(1, hs):
+        signal(barrier, head_dev(m))
+    for c in loads[4:]:
+        c.start()
+
+    def enter():
+        for n, below in ((0, z == 0), (1, z == 1), (2, z > 1)):
+            @pl.when(below)
+            def _(n=n):
+                pl.semaphore_wait(barrier, GROUP - 1 + hs - 1 + n)
+        for n in (1, 2):
+            @pl.when(z >= n)
+            def _(n=n):
+                signal(above, col_dev(-n))
+            @pl.when(z < n)
+            def _(n=n):
+                fin[n - 1] = jnp.zeros((FEAT, FEAT), f32)
+            @pl.when(z >= zs - n)
+            def _(n=n):
+                bin_[n - 1] = jnp.zeros((FEAT, FEAT), f32)
+
+    sent = []
+
+    def always(action):
+        action()
+
+    def remote(source, target, sends, receives, device, there=always, here=always):
         copy = pltpu.make_async_remote_copy(
             src_ref=source, dst_ref=target, send_sem=sends, recv_sem=receives,
             device_id=device, device_id_type=pl.DeviceIdType.MESH,
         )
-        copy.start()
-        return copy
+        there(copy.start)
+        sent.append((copy, there))
+        return lambda: here(copy.wait_recv)
+
+    def drain(copies):
+        for copy, there in copies:
+            there(copy.wait_send)
 
     def chunk(c):
         return pl.ds(c * ROWS, ROWS)
@@ -85,8 +119,8 @@
     def fade(rate, mask, count):
         return jnp.where(mask, jnp.exp(-rate * (BLK * jnp.maximum(count, 0.0))), 0.0)
 
-    for c in loads[4:]:
-        c.wait()
+    loads[2].wait()
+    loads[3].wait()
     b0 = (ctx * BLK).astype(f32)
     g0 = (z * (BLK * GROUP)).astype(f32)
     lens = jnp.broadcast_to(lens_ref[...].astype(f32), (128, 128))
@@ -149,17 +183,18 @@
         tail = jnp.where(tail_mask, jnp.exp(-rate_ref[0, h] * (BLK - 1.0 - t_row)), 0.0)
         fown[h] = nn((k_t * tail).astype(bf16), v_f.astype(bf16))
         if not a_copies:
-            pl.semaphore_wait(barrier, len(peers))
+            enter()
         if d:
             for c in range(CHUNKS):
                 a_copies[d, c] = remote(
                     fown.at[h, chunk(c)], frec.at[d, chunk(c)], a_s.at[d, c], a_r.at[d, c], row_dev(d)
                 )
 
-    loads[2].wait()
+    loads[4].wait()
     split_heads(qin, st_q)
-    loads[3].wait()
+    loads[5].wait()
     split_heads(gin, st_g)
+    loads[6].wait()
     gain_c = jnp.concatenate([gain_ref[...], jnp.zeros((FEAT - HPD, FEAT), f32)], axis=0).T
 
     s_col = lax.broadcasted_iota(jnp.int32, (BLK, BLK), 0).astype(f32)
@@ -193,17 +228,22 @@
         )
         for j in source
     ]
+    for n, over in ((1, z == zs - 2), (2, z < zs - 2)):
+        @pl.when(over)
+        def _(n=n):
+            pl.semaphore_wait(above, n)
     t_copies = {}
     for c in range(CHUNKS):
         for d in (1, 3, 2):
-            a_copies[d, c].wait()
+            a_copies[d, c]()
         total_c = coefs[0][GROUP : GROUP + 1, :] * fown[y, chunk(c), :]
         for d in range(1, GROUP):
             total_c = total_c + coefs[d][GROUP : GROUP + 1, :] * frec[d, chunk(c), :]
         fsum[chunk(c), :] = total_c
         for n in (1, 0):
             t_copies[n, c] = remote(
-                fsum.at[chunk(c)], fin.at[n, chunk(c)], t_s.at[n, c], t_r.at[n, c], col_dev(n + 1)
+                fsum.at[chunk(c)], fin.at[n, chunk(c)], t_s.at[n, c], t_r.at[n, c], col_dev(n + 1),
+                pl.when(z < zs - 1 - n), pl.when(z > n),
             )
     for i in range(1, GROUP):
         inner = coefs[0][i : i + 1, :] * fown[y]
@@ -217,11 +257,11 @@
     e_copies = {}
     for c in range(CHUNKS):
         for n in (0, 1):
-            t_copies[n, c].wait()
-        enter = fin[0, chunk(c), :] + far * fin[1, chunk(c), :]
-        fout[0, chunk(c), :] = enter
+            t_copies[n, c]()
+        entry = fin[0, chunk(c), :] + far * fin[1, chunk(c), :]
+        fout[0, chunk(c), :] = entry
         for i in range(1, GROUP):
-            fout[i, chunk(c), :] = fout[i, chunk(c), :] + carry[i : i + 1, :] * enter
+            fout[i, chunk(c), :] = fout[i, chunk(c), :] + carry[i : i + 1, :] * entry
         for d in (2, 1, 3):
             e_copies[d, c] = remote(
                 fout.at[(y + d) % GROUP, chunk(c)], fent.at[y, chunk(c)], e_s.at[d, c], e_r.at[d, c], row_dev(d)
@@ -234,7 +274,7 @@
         h = source[d]
         if d:
             for c in range(CHUNKS):
-                e_copies[d, c].wait()
+                e_copies[d, c]()
         state = fent[h].T.astype(bf16)
         o = oT[h] + in_row(h) * nn(state, qT[h])
         oT[h] = o
@@ -249,8 +289,8 @@
         remote(stat, stats.at[m], n_s.at[m], n_r.at[m], head_dev(m))
         for m in sorted(range(1, hs), key=lambda m: abs(m - hs // 2))
     ]
-    for c in n_copies:
-        c.wait()
+    for arrive in n_copies:
+        arrive()
     both = stat[...]
     for m in range(1, hs):
         both = both + stats[m]
@@ -259,6 +299,8 @@
     inv_row = jnp.concatenate([inverse[i : i + 1, :] for i in range(4)], axis=1)
     fac_row = jnp.concatenate([factor[i : i + 1, :] for i in range(4)], axis=1)
 
+    earlier = sent[:]
+    sent.clear()
     c_copies = {}
     for d in (2, 1, 3, 0):
         h = (y + d) % GROUP
@@ -285,6 +327,7 @@
         vacc[h, 0:256, :] = nt(probsT[h, 0:256, :], go)
         vacc[h, 256:512, :] = nt(probsT[h, 256:512, 256:], go[:, 256:])
 
+    drain(earlier)
     backward(0)
     backward(1)
     at = jnp.where(idx == 7, 0.0, idxf + 1.0)
@@ -296,14 +339,15 @@
     u_copies = {}
     for c in range(CHUNKS):
         for d in (1, 3, 2):
-            c_copies[d, c].wait()
+            c_copies[d, c]()
         total_c = coefs[0][7:8, :] * bown[y, chunk(c), :]
         for d in range(1, GROUP):
             total_c = total_c + coefs[d][7:8, :] * brec[d, chunk(c), :]
         bsum[chunk(c), :] = total_c
         for n in (1, 0):
             u_copies[n, c] = remote(
-                bsum.at[chunk(c)], bin_.at[n, chunk(c)], u_s.at[n, c], u_r.at[n, c], col_dev(-(n + 1))
+                bsum.at[chunk(c)], bin_.at[n, chunk(c)], u_s.at[n, c], u_r.at[n, c], col_dev(-(n + 1)),
+                pl.when(z > n), pl.when(z < zs - 1 - n),
             )
     for i in range(GROUP - 1):
         outer = coefs[0][i : i + 1, :] * bown[y]
@@ -315,28 +359,32 @@
     oq[...] = so_q[...].astype(bf16)
     far = fade(rate_y, first_g <= BLK * GROUP, jnp.full((8, 128), GROUP, f32))[6:7, :]
     carry = fade(rate_y, first_g[4:5, :] <= BLK * (idxf + 1.0), GROUP - 1.0 - idxf)
+    earlier = sent[:]
+    sent.clear()
     w_copies = {}
     for c in range(CHUNKS):
         for n in (0, 1):
-            u_copies[n, c].wait()
-        enter = bin_[0, chunk(c), :] + far * bin_[1, chunk(c), :]
-        bout[GROUP - 1, chunk(c), :] = enter
+            u_copies[n, c]()
+        entry = bin_[0, chunk(c), :] + far * bin_[1, chunk(c), :]
+        bout[GROUP - 1, chunk(c), :] = entry
         for i in range(GROUP - 1):
-            bout[i, chunk(c), :] = bout[i, chunk(c), :] + carry[i : i + 1, :] * enter
+            bout[i, chunk(c), :] = bout[i, chunk(c), :] + carry[i : i + 1, :] * entry
         for d in (2, 1, 3):
             w_copies[d, c] = remote(
                 bout.at[(y + d) % GROUP, chunk(c)], bent.at[y, chunk(c)], w_s.at[d, c], w_r.at[d, c], row_dev(d)
             )
     bent[y] = bout[y]
+    drain(earlier)
 
     for d in (0, 1, 3, 2):
         h = source[d]
         if d:
             for c in range(CHUNKS):
-                w_copies[d, c].wait()
+                w_copies[d, c]()
         state = bent[h].astype(bf16)
         so_k[pl.ds(h, BLK, stride=HPD), :] = kacc[h] + backc[h] * nt(vh[h], state)
         so_v[pl.ds(h, BLK, stride=HPD), :] = vacc[h] + backc[h] * nn(kh[h], state)
+    drain(sent)
     ok[...] = so_k[...].astype(bf16)
     ov[...] = so_v[...].astype(bf16)
 
@@ -378,7 +426,7 @@
     )
     dma = pltpu.SemaphoreType.DMA
     moves = [dma((GROUP, CHUNKS))] * 2 + [dma((2, CHUNKS))] * 2 + [dma((GROUP, CHUNKS))] * 2
-    sems = [dma((7,))] + moves + [dma((hs,))] * 2 + moves
+    sems = [dma((7,)), pltpu.SemaphoreType.REGULAR] + moves + [dma((hs,))] * 2 + moves
     operands = (*flat, gain, decay_rate.reshape(1, HPD), doc_lengths.reshape(1, doc_lengths.shape[0]))
     result = [jax.ShapeDtypeStruct((rows, FEAT), bf16)] * 3
     outs = pl.pallas_call(

time: 48.1 us -> 42.6 us (0.89)
  the two profiles are of different devices: /device:TPU:1 before, /device:TPU:192 now
where the time goes in v4:
time: 42.6 us; the launch traced here: 42.5 us
  Pallas kernels  41.8 us (98%)
  between operations  0.64 us (2%)
    pallas_call x1, Pallas kernels, local(): pl.pallas_call(functools.partial(kernel, zs, hs, zs * GROUP * BLK, hs * H...  40.7 us
    pallas_call x1, Pallas kernels, local(): pl.pallas_call(copy_out, out_shape=result, in_specs=[vmem] * 3, out_specs...  1.17 us

profile of v4, /device:TPU:192, one launch (start us, length us, event | category | flops | bytes accessed | tf_op | source)
XLA Modules:
  0.0 42.5 jit_solution(13143853496247830369)
XLA Ops:
  0.6 40.7 %shard_map.94 = (bf16[2048,128]{1,0:T(8,128)(2,1)S(1)}, bf16[2048,128]{1,0:T(8,128)(2,1)S(1)}, bf16[2048,128]{1,0:T(8,128)(2,1)S(1)}) custom-call(bf16[2048,128]{1,0:T(8,128)(2,1)} %bitcast.9, bf16[2048,128]{1,0:T(8,128)(2,1)} %bitcast.10, bf16[2048,128]{1,0:T(8,128)(2,1)} %bitcast.11, bf16[2048,128]{1,0:T(8,128)(2,1)} %bitcast.12, f32[4,128]{1,0:T(4,128)} %gain_hbm.1, ...), custom_call_target="tpu_custom_call" | custom-call | flops 2000000000 | bytes 4000000 | tf_op jit(solution)/shard_map/pallas_call | solution.py:432
  41.3 1.2 %shard_map.95 = (bf16[2048,128]{1,0:T(8,128)(2,1)}, bf16[2048,128]{1,0:T(8,128)(2,1)}, bf16[2048,128]{1,0:T(8,128)(2,1)}) custom-call(bf16[2048,128]{1,0:T(8,128)(2,1)S(1)} %get-tuple-element.9.a, bf16[2048,128]{1,0:T(8,128)(2,1)S(1)} %get-tuple-element.10.b, bf16[2048,128]{1,0:T(8,128)(2,1)S(1)} %get-tuple-element.11.c), custom_call_target="tpu_custom_call" | custom-call | tf_op jit(solution)/shard_map/pallas_call | solution.py:443

commit v5 on v4

--- a/solution.py
+++ b/solution.py
@@ -299,20 +299,24 @@
     inv_row = jnp.concatenate([inverse[i : i + 1, :] for i in range(4)], axis=1)
     fac_row = jnp.concatenate([factor[i : i + 1, :] for i in range(4)], axis=1)
 
-    earlier = sent[:]
-    sent.clear()
-    c_copies = {}
-    for d in (2, 1, 3, 0):
-        h = (y + d) % GROUP
+    def gradient_state(h):
         go = (gT[h] * inv_row - oT[h] * fac_row).astype(bf16)
         goT[h] = go
         lead = jnp.where(lead_mask, jnp.exp(-rate_ref[0, h] * t_row), 0.0)
         bown[h] = nt((qT[h].astype(f32) * lead).astype(bf16), go)
-        if d:
-            for c in range(CHUNKS):
-                c_copies[d, c] = remote(
-                    bown.at[h, chunk(c)], brec.at[d, chunk(c)], c_s.at[d, c], c_r.at[d, c], row_dev(d)
-                )
+
+    for d in (2, 1, 3):
+        gradient_state((y + d) % GROUP)
+    earlier = sent[:]
+    sent.clear()
+    c_copies = {}
+    for c in range(CHUNKS):
+        for d in (2, 1, 3):
+            h = (y + d) % GROUP
+            c_copies[d, c] = remote(
+                bown.at[h, chunk(c)], brec.at[d, chunk(c)], c_s.at[d, c], c_r.at[d, c], row_dev(d)
+            )
+    gradient_state(y)
 
     def backward(h):
         go = goT[h]

time: 42.6 us -> 42.2 us (level)
  the two profiles are of different devices: /device:TPU:192 before, /device:TPU:64 now
where the time goes in v5:
time: 42.2 us; the launch traced here: 42 us
  Pallas kernels  41.4 us (98%)
  between operations  0.64 us (2%)
    pallas_call x1, Pallas kernels, local(): pl.pallas_call(functools.partial(kernel, zs, hs, zs * GROUP * BLK, hs * H...  40.2 us
    pallas_call x1, Pallas kernels, local(): pl.pallas_call(copy_out, out_shape=result, in_specs=[vmem] * 3, out_specs...  1.17 us

profile of v5, /device:TPU:64, one launch (start us, length us, event | category | flops | bytes accessed | tf_op | source)
XLA Modules:
  0.0 42.0 jit_solution(15146479276855184494)
XLA Ops:
  0.6 40.2 %shard_map.94 = (bf16[2048,128]{1,0:T(8,128)(2,1)S(1)}, bf16[2048,128]{1,0:T(8,128)(2,1)S(1)}, bf16[2048,128]{1,0:T(8,128)(2,1)S(1)}) custom-call(bf16[2048,128]{1,0:T(8,128)(2,1)} %bitcast.9, bf16[2048,128]{1,0:T(8,128)(2,1)} %bitcast.10, bf16[2048,128]{1,0:T(8,128)(2,1)} %bitcast.11, bf16[2048,128]{1,0:T(8,128)(2,1)} %bitcast.12, f32[4,128]{1,0:T(4,128)} %gain_hbm.1, ...), custom_call_target="tpu_custom_call" | custom-call | flops 2000000000 | bytes 4000000 | tf_op jit(solution)/shard_map/pallas_call | solution.py:436
  40.9 1.2 %shard_map.95 = (bf16[2048,128]{1,0:T(8,128)(2,1)}, bf16[2048,128]{1,0:T(8,128)(2,1)}, bf16[2048,128]{1,0:T(8,128)(2,1)}) custom-call(bf16[2048,128]{1,0:T(8,128)(2,1)S(1)} %get-tuple-element.9.a, bf16[2048,128]{1,0:T(8,128)(2,1)S(1)} %get-tuple-element.10.b, bf16[2048,128]{1,0:T(8,128)(2,1)S(1)} %get-tuple-element.11.c), custom_call_target="tpu_custom_call" | custom-call | tf_op jit(solution)/shard_map/pallas_call | solution.py:447

commit v6 on v5

--- a/solution.py
+++ b/solution.py
@@ -162,7 +162,7 @@
         return jnp.where(in_mask, jnp.exp(-rate_ref[0, h] * (t_row + 1.0)), 0.0)
 
     def split_heads(source, stage):
-        stage[...] = source[...].astype(f32)
+        stage[0 : BLK * HPD, :] = source[...].astype(f32)
 
     def of_head(stage, h):
         return stage[pl.ds(h, BLK, stride=HPD), :]
@@ -360,7 +360,7 @@
         bout[i] = outer
     backward(2)
     backward(3)
-    oq[...] = so_q[...].astype(bf16)
+    oq[...] = so_q[0 : BLK * HPD, :].astype(bf16)
     far = fade(rate_y, first_g <= BLK * GROUP, jnp.full((8, 128), GROUP, f32))[6:7, :]
     carry = fade(rate_y, first_g[4:5, :] <= BLK * (idxf + 1.0), GROUP - 1.0 - idxf)
     earlier = sent[:]
@@ -389,8 +389,8 @@
         so_k[pl.ds(h, BLK, stride=HPD), :] = kacc[h] + backc[h] * nt(vh[h], state)
         so_v[pl.ds(h, BLK, stride=HPD), :] = vacc[h] + backc[h] * nn(kh[h], state)
     drain(sent)
-    ok[...] = so_k[...].astype(bf16)
-    ov[...] = so_v[...].astype(bf16)
+    ok[...] = so_k[0 : BLK * HPD, :].astype(bf16)
+    ov[...] = so_v[0 : BLK * HPD, :].astype(bf16)
 
 
 def copy_out(a, b, c, a_hbm, b_hbm, c_hbm, sems):
@@ -417,7 +417,7 @@
     ]
     scratch = (
         [V((rows, FEAT), bf16)] * 4
-        + [V((rows, FEAT), f32)] * 4
+        + [V((rows + 8, FEAT), f32)] * 4
         + [V((HPD, BLK, FEAT), bf16)] * 3
         + [V((HPD, FEAT, BLK), bf16)] * 3
         + [V((HPD, FEAT, BLK), f32), V((BLK, BLK), f32), V((HPD, BLK, BLK), f32), V((HPD, BLK, BLK), bf16)]
@@ -425,7 +425,7 @@
         + chain + chain
         + [V((8, 128), f32), V((hs, 8, 128), f32)]
         + [V((HPD, BLK, FEAT), f32)] * 3
-        + [V((rows, FEAT), f32)] * 3
+        + [V((rows + 8, FEAT), f32)] * 3
         + [V((HPD, FEAT), f32), pltpu.SMEM((1, HPD), f32), V((1, doc_lengths.shape[0]), jnp.int32)]
     )
     dma = pltpu.SemaphoreType.DMA

time: 42.2 us -> 42.2 us (level)
  no operation moved by 1% of the time
where the time goes in v6:
time: 42.2 us; the launch traced here: 42 us
  Pallas kernels  41.4 us (98%)
  between operations  0.64 us (2%)
    pallas_call x1, Pallas kernels, local(): pl.pallas_call(functools.partial(kernel, zs, hs, zs * GROUP * BLK, hs * H...  40.2 us
    pallas_call x1, Pallas kernels, local(): pl.pallas_call(copy_out, out_shape=result, in_specs=[vmem] * 3, out_specs...  1.17 us

profile of v6, /device:TPU:64, one launch (start us, length us, event | category | flops | bytes accessed | tf_op | source)
XLA Modules:
  0.0 42.0 jit_solution(5379800186606389631)
XLA Ops:
  0.6 40.2 %shard_map.94 = (bf16[2048,128]{1,0:T(8,128)(2,1)S(1)}, bf16[2048,128]{1,0:T(8,128)(2,1)S(1)}, bf16[2048,128]{1,0:T(8,128)(2,1)S(1)}) custom-call(bf16[2048,128]{1,0:T(8,128)(2,1)} %bitcast.9, bf16[2048,128]{1,0:T(8,128)(2,1)} %bitcast.10, bf16[2048,128]{1,0:T(8,128)(2,1)} %bitcast.11, bf16[2048,128]{1,0:T(8,128)(2,1)} %bitcast.12, f32[4,128]{1,0:T(4,128)} %gain_hbm.1, ...), custom_call_target="tpu_custom_call" | custom-call | flops 2000000000 | bytes 4000000 | tf_op jit(solution)/shard_map/pallas_call | solution.py:436
  40.9 1.2 %shard_map.95 = (bf16[2048,128]{1,0:T(8,128)(2,1)}, bf16[2048,128]{1,0:T(8,128)(2,1)}, bf16[2048,128]{1,0:T(8,128)(2,1)}) custom-call(bf16[2048,128]{1,0:T(8,128)(2,1)S(1)} %get-tuple-element.9.a, bf16[2048,128]{1,0:T(8,128)(2,1)S(1)} %get-tuple-element.10.b, bf16[2048,128]{1,0:T(8,128)(2,1)S(1)} %get-tuple-element.11.c), custom_call_target="tpu_custom_call" | custom-call | tf_op jit(solution)/shard_map/pallas_call | solution.py:447
